TPU v7x, 128 devices: a whole 4x4x4 slice. The times are simulated.
128 devices in a mesh: inst: 8 (over x_hi, y), tp: 16 (over z, x_lo, core).
Axes of the slice: x: 4 (x_hi: 2, x_lo: 2; x = x_hi * 2 + x_lo), y: 4, z: 4, core: 2. Of those that a mesh axis runs over, the one named last changes fastest.
Arguments:
- cache_pool: bfloat16 [1536, 2, 8, 128, 128], P(('inst', 'tp')), may hold values from -20 to 20
- first_query: bfloat16 [32, 16384], P('inst', 'tp'), may hold values from -23 to 23
- second_query: bfloat16 [32, 16384], P('inst', 'tp'), may hold values from -23 to 23
- first_fresh: bfloat16 [32, 2, 1024], P('inst'), may hold values from -5 to 5
- second_fresh: bfloat16 [32, 2, 1024], P('inst'), may hold values from -5 to 5
- first_tables: int32 [32, 32], P('inst'), may hold values from 0 to 191, as said below
- second_tables: int32 [32, 32], P('inst'), may hold values from 0 to 191, as said below
- first_lengths: int32 [32], P('inst'), may hold values from 1 to 4094
- second_lengths: int32 [32], P('inst'), may hold values from 2 to 4095, as said below
- page_moves: int32 [128, 8, 2, 2], P(('inst', 'tp')), may hold values from -1 to 10, as said below
Outputs:
- first_output: bfloat16 [32, 16384], P('inst', 'tp')
- second_output: bfloat16 [32, 16384], P('inst', 'tp')
- cache_after: bfloat16 [1536, 2, 8, 128, 128], P(('inst', 'tp'))
Inputs may be any that keep to these rules, and one draw needn't show every extreme that they name: `first_tables`: row s lists the 32 slots reserved for session s in its instance, as t * 12 + l for local slot l of the instance's device with tp index t; the entries of one instance all differ. `second_tables`: rows of sessions that stay equal their first_tables rows; a session that arrived takes the slot of a session that left, and its row names slots that page_moves fills and that no row of first_tables names, each on the device with the same tp index as the page's source slot. `second_lengths`: one more than the first length of the same session: the one that stayed, or for an arrived session the one it came from. `page_moves`: instance i hands exactly one session to each instance (i + r) mod 8 for r = 1 to 2, with all its pages up to its first length; entry [d, b, c] is (source local slot on device d, target local slot on the device of instance b with d's tp index), unused entries are (-1, -1), rows of all other instances are unused; no slot is written twice, and no written slot is a source.
All inputs are finite; a program needn't handle non-finite values.
Results may differ from a plain program's by a relative error of at most 0.0029.
Values may be sent and summed in bfloat16 or wider, within the bound.
A program may use at most 128 MiB of HBM per device.

v0:
```python
import jax
import jax.numpy as jnp
from jax import lax
from jax.sharding import PartitionSpec as P

HEADS = 128
KVH = 8
HD = 128
PAGE = 128
MIG = 2


def joined(value, axis, join):
    pieces = jax.tree.map(lambda part: lax.all_gather(part, axis), value)
    head = jax.tree.map(lambda part: part[0], pieces)
    tail = jax.tree.map(lambda part: part[1:], pieces)
    so_far, _ = lax.scan(lambda so_far, piece: (join(so_far, piece), None), head, tail)
    return so_far


def from_behind(value, axis, steps):
    count = lax.axis_size(axis)
    pairs = [(source, (source + steps) % count) for source in range(count)]
    return lax.ppermute(value, axis, pairs)


def append_token(cache, tables, lengths, fresh, tp_index):
    slots_here = cache.shape[0]
    named = jnp.take_along_axis(tables, (lengths // PAGE)[:, None], 1)[:, 0]
    local_slot = jnp.where(named // slots_here == tp_index, named % slots_here, slots_here)
    values = fresh.reshape(fresh.shape[0], 2, KVH, HD)
    return cache.at[local_slot, :, :, lengths % PAGE, :].set(values, mode="drop")


def page_terms(cache, queries, tables, lengths, slot_ids):
    pages_here = cache.shape[0]
    page_index = jnp.arange(tables.shape[1], dtype=jnp.int32)
    live_pages = page_index[None, :] <= (lengths // PAGE)[:, None]
    matches = (tables[None, :, :] == slot_ids[:, None, None]) & live_pages[None, :, :]
    owners = jnp.any(matches, axis=2)
    page_number = jnp.sum(jnp.where(matches, page_index[None, None, :], 0), axis=(1, 2))
    last_token = jnp.sum(jnp.where(owners, lengths[None, :], 0), axis=1)
    in_use = jnp.any(owners, axis=1)
    picked = jnp.dot(
        owners.astype(jnp.bfloat16), queries, preferred_element_type=jnp.float32
    ).astype(jnp.bfloat16)
    picked = picked.reshape(pages_here, KVH, HEADS // KVH, HD)
    scores = jnp.einsum(
        "pkgd,pktd->pkgt", picked, cache[:, 0], preferred_element_type=jnp.float32
    ) * HD ** (-0.5)
    position = page_number[:, None] * PAGE + jnp.arange(PAGE, dtype=jnp.int32)[None, :]
    visible = (in_use[:, None] & (position <= last_token[:, None]))[:, None, None, :]
    page_top = jnp.max(jnp.where(visible, scores, -1e30), axis=3)
    weights = jnp.where(visible, jnp.exp(scores - page_top[..., None]), 0.0)
    page_sum = jnp.einsum(
        "pkgt,pktd->pkgd",
        weights.astype(jnp.bfloat16),
        cache[:, 1],
        preferred_element_type=jnp.float32,
    )
    page_total = jnp.sum(weights, axis=3).reshape(pages_here, HEADS)
    page_top = page_top.reshape(pages_here, HEADS)
    page_sum = page_sum.reshape(pages_here, HEADS, HD)
    local_top = jnp.max(jnp.where(owners[:, :, None], page_top[:, None, :], -1e30), axis=0)
    factor = jnp.where(
        owners[:, :, None], jnp.exp(page_top[:, None, :] - local_top[None, :, :]), 0.0
    )
    local_sum = jnp.einsum("psh,phd->shd", factor, page_sum, precision=lax.Precision.HIGHEST)
    local_total = jnp.einsum("psh,ph->sh", factor, page_total, precision=lax.Precision.HIGHEST)
    return (local_top, local_sum, local_total)


def join_parts(one_side, other_side):
    overall = jnp.maximum(one_side[0], other_side[0])
    one_scale = jnp.exp(one_side[0] - overall)
    other_scale = jnp.exp(other_side[0] - overall)
    summed = one_side[1] * one_scale[:, :, None] + other_side[1] * other_scale[:, :, None]
    totals = one_side[2] * one_scale + other_side[2] * other_scale
    return (overall, summed, totals)


def decode(cache, query, tables, lengths, tp_index):
    queries = lax.all_gather(query, "tp", axis=1, tiled=True)
    slot_ids = tp_index * cache.shape[0] + jnp.arange(cache.shape[0], dtype=jnp.int32)
    local_top, local_sum, local_total = page_terms(cache, queries, tables, lengths, slot_ids)
    own_heads = query.shape[1] // HD
    overall, summed, totals = joined((local_top, local_sum, local_total), "tp", join_parts)
    summed = lax.dynamic_slice_in_dim(summed, tp_index * own_heads, own_heads, 1)
    totals = lax.dynamic_slice_in_dim(totals, tp_index * own_heads, own_heads, 1)
    return (
        (summed / totals[:, :, None]).reshape(query.shape[0], own_heads * HD).astype(jnp.bfloat16)
    )


def migrate(cache, page_moves):
    move_plan = page_moves[0]
    slots_here = cache.shape[0]
    instances = lax.axis_size("inst")
    own_inst = lax.axis_index("inst")
    for offset in range(1, MIG + 1):
        send_rows = lax.dynamic_index_in_dim(
            move_plan, (own_inst + offset) % instances, 0, keepdims=False
        )
        payload = cache[jnp.maximum(send_rows[:, 0], 0)]
        arrived, target_slots = from_behind((payload, send_rows[:, 1]), "inst", offset)
        cache = cache.at[jnp.where(target_slots >= 0, target_slots, slots_here)].set(
            arrived, mode="drop"
        )
    return cache


def shards(
    cache_pool,
    first_query,
    second_query,
    first_fresh,
    second_fresh,
    first_tables,
    second_tables,
    first_lengths,
    second_lengths,
    page_moves,
):
    tp_index = lax.axis_index("tp")
    cache = append_token(cache_pool, first_tables, first_lengths, first_fresh, tp_index)
    first_output = decode(cache, first_query, first_tables, first_lengths, tp_index)
    cache = migrate(cache, page_moves)
    cache = append_token(cache, second_tables, second_lengths, second_fresh, tp_index)
    second_output = decode(cache, second_query, second_tables, second_lengths, tp_index)
    return (first_output, second_output, cache)


def solution(mesh):
    placed = (
        P(("inst", "tp"), None, None, None, None),
        P("inst", "tp"),
        P("inst", "tp"),
        P("inst", None, None),
        P("inst", None, None),
        P("inst", None),
        P("inst", None),
        P("inst"),
        P("inst"),
        P(("inst", "tp"), None, None, None),
    )
    return jax.shard_map(
        shards,
        mesh=mesh,
        in_specs=placed,
        out_specs=(P("inst", "tp"), P("inst", "tp"), P(("inst", "tp"), None, None, None, None)),
        check_vma=False,
    )
```

profile of v0, /device:TPU:27, one launch (start us, length us, event | category | flops | bytes accessed | tf_op | source)
XLA Modules:
  0.0 304.5 jit_solution(9379360489891942054)
XLA Ops:
  7.3 8.1 %copy.148 = bf16[12,2,8,128,128]{4,3,2,1,0:T(8,128)(2,1)} copy(bf16[12,2,8,128,128]{4,3,2,1,0:T(8,128)(2,1)} %param.16) | data formatting | bytes 12582912
  16.9 18.7 %all_gather.42 = bf16[4,16384]{1,0:T(4,128)(2,1)S(1)} all-gather(bf16[4,1024]{1,0:T(4,128)(2,1)S(1)} %copy-done.10), channel_id=1, replica_groups=mesh['inst'=8,'tp'=16] {'tp'}, dimensions={1}, use_global_device_ids=true | all-gather | bytes 139264 | tf_op jit(solution)/shard_map/all_gather | solution.py:83
  37.5 2.2 scatter_fusion
  39.7 3.7 %select_reduce_fusion.1 = (f32[12,8,16]{2,1,0:T(8,128)S(1)}, f32[12,8,16,128]{3,2,1,0:T(8,128)S(1)}) fusion(pred[12,128]{1,0:T(8,128)(4,1)S(1)} %fusion.36, bf16[12,8,16,128]{3,2,1,0:T(8,128)(2,1)S(1)} %bitcast.175, bf16[12,2,8,128,128]{4,3,2,1,0:T(8,128)(2,1)} %scatter_fusion), kind=kOutput, calls=%fused_computation.43 | convolution fusion | flops 50919936 | bytes 4333056 | tf_op jit(solution)/shard_map/pkgd,pktd->pkgt/dot_general | solution.py:48
  43.5 2.9 fusion.6
  46.6 1.7 convolution_bitcast_fusion.1
  49.6 2.2 collective-permute-start
  51.8 3.5 %gather_fusion = bf16[2,2,8,128,128]{4,3,2,1,0:T(8,128)(2,1)S(1)} fusion(bf16[12,2,8,128,128]{4,3,2,1,0:T(8,128)(2,1)} %scatter_fusion, s32[1024]{0:T(1024)S(1)} %pad_clamp_fusion.1), kind=kCustom, calls=%fused_computation.2 | custom fusion | bytes 2097160 | tf_op jit(solution)/shard_map/gather | solution.py:104
  57.1 2.0 collective-permute-start.2
  60.5 52.5 %all_gather.49 = bf16[4,16384]{1,0:T(4,128)(2,1)S(1)} all-gather(bf16[4,1024]{1,0:T(4,128)(2,1)S(1)} %copy-done.11), channel_id=1, replica_groups=mesh['inst'=8,'tp'=16] {'tp'}, dimensions={1}, use_global_device_ids=true | all-gather | bytes 139264 | tf_op jit(solution)/shard_map/all_gather | solution.py:83
  113.8 2.6 scatter_fusion.1
  116.5 3.5 %gather_fusion.1 = bf16[2,2,8,128,128]{4,3,2,1,0:T(8,128)(2,1)S(1)} fusion(bf16[12,2,8,128,128]{4,3,2,1,0:T(8,128)(2,1)} %scatter_fusion.1, s32[1024]{0:T(1024)S(1)} %pad_clamp_fusion), kind=kCustom, calls=%fused_computation.3 | custom fusion | bytes 2097160 | tf_op jit(solution)/shard_map/gather | solution.py:104
  120.7 37.1 %all-gather.6 = f32[16,4,128]{2,1,0:T(4,128)S(1)} all-gather(f32[1,4,128]{2,1,0:T(4,128)S(1)} %copy.66), channel_id=2, replica_groups=mesh['inst'=8,'tp'=16] {'tp'}, dimensions={0}, use_global_device_ids=true | all-gather | bytes 34816 | tf_op jit(solution)/shard_map/all_gather | solution.py:14
  157.8 21.1 %all-gather.7 = f32[16,4,128]{2,1,0:T(4,128)S(1)} all-gather(f32[1,4,128]{2,1,0:T(4,128)S(1)} %bitcast.186), channel_id=4, replica_groups=mesh['inst'=8,'tp'=16] {'tp'}, dimensions={0}, use_global_device_ids=true | all-gather | bytes 34816 | tf_op jit(solution)/shard_map/all_gather | solution.py:14
  180.6 2.8 scatter_fusion.2
  183.3 11.2 %copy.71 = bf16[12,2,8,128,128]{4,2,3,1,0:T(8,128)(2,1)} copy(bf16[12,2,8,128,128]{4,3,2,1,0:T(8,128)(2,1)} %scatter_fusion.2) | data formatting | bytes 12582912 | tf_op jit(solution)/shard_map/scatter | solution.py:106
  194.5 1.4 scatter_fusion.3
  195.9 7.5 %copy.78 = bf16[12,2,8,128,128]{4,3,2,1,0:T(8,128)(2,1)} copy(bf16[12,2,8,128,128]{4,2,3,1,0:T(8,128)(2,1)} %scatter_fusion.3) | data formatting | bytes 12582912
  203.9 3.3 %select_reduce_fusion = (f32[12,8,16]{2,1,0:T(8,128)}, f32[12,8,16,128]{3,2,1,0:T(8,128)}) fusion(pred[12,128]{1,0:T(8,128)(4,1)S(1)} %fusion.37, bf16[12,8,16,128]{3,2,1,0:T(8,128)(2,1)S(1)} %bitcast.174, bf16[12,1,8,128,128]{4,2,3,1,0:T(8,128)(2,1)S(1)} %get-tuple-element.179), kind=kOutput, calls=%fused_computation.41 | convolution fusion | flops 50919936 | bytes 4333056 | tf_op jit(solution)/shard_map/pkgd,pktd->pkgt/dot_general | solution.py:48
  208.4 2.1 fusion.8
  210.6 1.7 convolution_bitcast_fusion
  213.0 1.7 fusion.16
  215.3 16.4 %all-gather.8 = f32[16,4,128]{2,1,0:T(4,128)S(1)} all-gather(f32[1,4,128]{2,1,0:T(4,128)S(1)} %copy.74), channel_id=5, replica_groups=mesh['inst'=8,'tp'=16] {'tp'}, dimensions={0}, use_global_device_ids=true | all-gather | bytes 34816 | tf_op jit(solution)/shard_map/all_gather | solution.py:14
  231.7 17.7 %all-gather.9 = f32[16,4,128]{2,1,0:T(4,128)S(1)} all-gather(f32[1,4,128]{2,1,0:T(4,128)S(1)} %bitcast.187), channel_id=7, replica_groups=mesh['inst'=8,'tp'=16] {'tp'}, dimensions={0}, use_global_device_ids=true | all-gather | bytes 34816 | tf_op jit(solution)/shard_map/all_gather | solution.py:14
  249.5 4.5 %slice.122 = f32[60,128,128]{2,1,0:T(8,128)} slice(f32[64,128,128]{2,1,0:T(8,128)} %all-gather.13.cloned.1.call-done), slice={[4:64], [0:128], [0:128]} | slice | bytes 7864320 | tf_op jit(solution)/shard_map/slice | solution.py:16
  254.0 18.8 %while.28 = (s32[]{:T(128)}, f32[4,128]{1,0:T(4,128)S(1)}, f32[4,128,128]{2,1,0:T(8,128)S(1)}, f32[4,128]{1,0:T(4,128)S(1)}, f32[15,4,128]{2,1,0:T(4,128)S(1)}, ...) while((s32[]{:T(128)}, f32[4,128]{1,0:T(4,128)S(1)}, ...), condition=%wide.region_9.11_spmd, body=%wide.region_8.10_spmd.sunk | while | flops 199682 | bytes 807013 | solution.py:17
  254.1 1.2 fusion.68
  255.3 1.2 fusion.68
  256.6 1.2 fusion.68
  257.8 1.2 fusion.68
  260.3 1.2 fusion.68
  261.6 1.2 fusion.68
  264.1 1.2 fusion.68
  265.3 1.2 fusion.68
  266.6 1.2 fusion.68
  267.8 1.2 fusion.68
  270.3 1.2 fusion.68
  271.6 1.2 fusion.68
  273.6 4.5 %slice.130 = f32[60,128,128]{2,1,0:T(8,128)} slice(f32[64,128,128]{2,1,0:T(8,128)} %all-gather.15.cloned.1.call-done), slice={[4:64], [0:128], [0:128]} | slice | bytes 7864320 | tf_op jit(solution)/shard_map/slice | solution.py:16
  278.1 18.8 %while.29 = (s32[]{:T(128)}, f32[4,128]{1,0:T(4,128)S(1)}, f32[4,128,128]{2,1,0:T(8,128)S(1)}, f32[4,128]{1,0:T(4,128)S(1)}, f32[15,4,128]{2,1,0:T(4,128)S(1)}, ...) while((s32[]{:T(128)}, f32[4,128]{1,0:T(4,128)S(1)}, ...), condition=%wide.region_21.23_spmd, body=%wide.region_20.22_spmd.sunk | while | flops 199682 | bytes 807013 | solution.py:17
  278.1 1.2 fusion.70
  279.4 1.2 fusion.70
  280.6 1.2 fusion.70
  281.9 1.2 fusion.70
  283.1 1.2 fusion.70
  284.4 1.2 fusion.70
  286.9 1.2 fusion.70
  288.1 1.2 fusion.70
  (160 shorter events, 28.6 us)
Async XLA Ops:
  7.2 9.8 %copy-start.10 = (bf16[4,1024]{1,0:T(4,128)(2,1)S(1)}, bf16[4,1024]{1,0:T(4,128)(2,1)}, u32[]{:S(2)}) copy-start(bf16[4,1024]{1,0:T(4,128)(2,1)} %param.17) | copy-start | bytes 24580
  7.2 29.6 %copy-start.8 = (bf16[4,2,1024]{2,1,0:T(2,128)(2,1)S(1)}, bf16[4,2,1024]{2,1,0:T(2,128)(2,1)}, u32[]{:S(2)}) copy-start(bf16[4,2,1024]{2,1,0:T(2,128)(2,1)} %param.19) | copy-start | bytes 49156
  7.2 8.4 %copy-start = (s32[4,32]{1,0:T(4,128)S(1)}, s32[4,32]{1,0:T(4,128)}, u32[]{:S(2)}) copy-start(s32[4,32]{1,0:T(4,128)} %param.21) | copy-start | bytes 1540
  7.2 8.4 %copy-start.1 = (s32[4,32]{1,0:T(4,128)S(1)}, s32[4,32]{1,0:T(4,128)}, u32[]{:S(2)}) copy-start(s32[4,32]{1,0:T(4,128)} %param.22) | copy-start | bytes 1540
  7.2 8.3 %copy-start.13 = (s32[4]{0:T(128)S(1)}, s32[4]{0:T(128)}, u32[]{:S(2)}) copy-start(s32[4]{0:T(128)} %param.23) | copy-start | bytes 52
  7.2 8.2 %copy-start.14 = (s32[4]{0:T(128)S(1)}, s32[4]{0:T(128)}, u32[]{:S(2)}) copy-start(s32[4]{0:T(128)} %param.24) | copy-start | bytes 52
  7.2 242.2 %all-gather.13.cloned.1.call-start = ((), (), s32[]{:S(2)}) async-start(), calls=%async_computation | async-start | bytes 4456448 | tf_op jit(solution)/shard_map/all_gather | solution.py:14
  36.1 13.0 %copy-start.12 = (s32[1,8,2,2]{1,3,2,0:T(2,128)S(1)}, s32[1,8,2,2]{1,3,2,0:T(2,128)}, u32[]{:S(2)}) copy-start(s32[1,8,2,2]{1,3,2,0:T(2,128)} %param.25) | copy-start | bytes 388
  43.4 17.1 %copy-start.11 = (bf16[4,1024]{1,0:T(4,128)(2,1)S(1)}, bf16[4,1024]{1,0:T(4,128)(2,1)}, u32[]{:S(2)}) copy-start(bf16[4,1024]{1,0:T(4,128)(2,1)} %param.18) | copy-start | bytes 24580
  49.1 129.9 %copy-start.9 = (bf16[4,2,1024]{2,1,0:T(2,128)(2,1)S(1)}, bf16[4,2,1024]{2,1,0:T(2,128)(2,1)}, u32[]{:S(2)}) copy-start(bf16[4,2,1024]{2,1,0:T(2,128)(2,1)} %param.20) | copy-start | bytes 49156
  49.1 224.5 %all-gather.15.cloned.1.call-start = ((), (), s32[]{:S(2)}) async-start(), calls=%async_computation.1 | async-start | bytes 4456448 | tf_op jit(solution)/shard_map/all_gather | solution.py:14
  49.6 64.2 %collective-permute-start = (s32[2]{0:T(128)S(1)}, s32[2]{0:T(128)S(1)}, u32[]{:S(2)}, u32[]{:S(2)}) collective-permute-start(s32[2]{0:T(128)S(1)} %get-tuple-element.133), channel_id=1, source_target_pairs={{0,16},{16,32},{32,48},{48,64},{64,80},{80,96},{96,112},{112,0},{1... | collective-permute-start | bytes 32 | tf_op jit(solution)/shard_map/ppermute | solution.py:24
  55.4 58.5 %collective-permute-start.1 = (bf16[2,2,8,128,128]{4,3,2,1,0:T(8,128)(2,1)S(1)}, bf16[2,2,8,128,128]{4,3,2,1,0:T(8,128)(2,1)S(1)}, u32[]{:S(2)}, u32[]{:S(2)}) collective-permute-start(bf16[2,2,8,128,128]{4,3,2,1,0:T(8,128)(2,1)S(1)} %gather_fusion), channel_id=1, source_target_pairs={{0,16},{16,32},{32,48},{48,64},{64,80},{80,96},{96,112},{112,0},{1... | collective-permute-start | bytes 3145736 | tf_op jit(solution)/shard_map/ppermute | solution.py:24
  57.1 122.8 %collective-permute-start.2 = (s32[2]{0:T(128)}, s32[2]{0:T(128)}, u32[]{:S(2)}, u32[]{:S(2)}) collective-permute-start(s32[2]{0:T(128)} %get-tuple-element.131), channel_id=1, source_target_pairs={{0,32},{16,48},{32,64},{48,80},{64,96},{80,112},{96,0},{112,16},{1... | collective-permute-start | bytes 32 | tf_op jit(solution)/shard_map/ppermute | solution.py:24
  120.0 60.6 %collective-permute-start.3 = (bf16[2,2,8,128,128]{4,3,2,1,0:T(8,128)(2,1)S(1)}, bf16[2,2,8,128,128]{4,3,2,1,0:T(8,128)(2,1)S(1)}, u32[]{:S(2)}, u32[]{:S(2)}) collective-permute-start(bf16[2,2,8,128,128]{4,3,2,1,0:T(8,128)(2,1)S(1)} %gather_fusion.1), channel_id=1, source_target_pairs={{0,32},{16,48},{32,64},{48,80},{64,96},{80,112},{96,0},{112,16},{1... | collective-permute-start | bytes 3145736 | tf_op jit(solution)/shard_map/ppermute | solution.py:24
  157.8 36.7 %copy-start.4 = (f32[16,4,128]{2,1,0:T(4,128)}, f32[16,4,128]{2,1,0:T(4,128)S(1)}, u32[]{:S(2)}) copy-start(f32[16,4,128]{2,1,0:T(4,128)S(1)} %all-gather.6) | copy-start | bytes 98308
  178.8 15.7 %copy-start.5 = (f32[16,4,128]{2,1,0:T(4,128)}, f32[16,4,128]{2,1,0:T(4,128)S(1)}, u32[]{:S(2)}) copy-start(f32[16,4,128]{2,1,0:T(4,128)S(1)} %all-gather.7) | copy-start | bytes 98308
  195.9 7.6 %copy-start.2 = (bf16[12,2,8,128,128]{4,2,3,1,0:T(8,128)(2,1)S(1)}, bf16[12,2,8,128,128]{4,2,3,1,0:T(8,128)(2,1)}, u32[]{:S(2)}) copy-start(bf16[12,2,8,128,128]{4,2,3,1,0:T(8,128)(2,1)} %scatter_fusion.3) | copy-start | bytes 18874372
  207.2 5.9 %copy-start.3 = (f32[12,8,16]{2,1,0:T(8,128)S(1)}, f32[12,8,16]{2,1,0:T(8,128)}, u32[]{:S(2)}) copy-start(f32[12,8,16]{2,1,0:T(8,128)} %get-tuple-element.186) | copy-start | bytes 18436
  210.6 43.4 %slice-start.2 = ((f32[16,4,128]{2,1,0:T(4,128)}), f32[15,4,128]{2,1,0:T(4,128)S(1)}, s32[]{:S(2)}) async-start(f32[16,4,128]{2,1,0:T(4,128)} %copy-done.4), calls=%async_computation.4 | async-start | bytes 61440 | tf_op jit(solution)/shard_map/slice | solution.py:16
  210.6 43.4 %slice-start.3 = ((f32[16,4,128]{2,1,0:T(4,128)}), f32[15,4,128]{2,1,0:T(4,128)S(1)}, s32[]{:S(2)}) async-start(f32[16,4,128]{2,1,0:T(4,128)} %copy-done.5), calls=%async_computation.5 | async-start | bytes 61440 | tf_op jit(solution)/shard_map/slice | solution.py:16
  231.7 22.3 %copy-start.6 = (f32[16,4,128]{2,1,0:T(4,128)}, f32[16,4,128]{2,1,0:T(4,128)S(1)}, u32[]{:S(2)}) copy-start(f32[16,4,128]{2,1,0:T(4,128)S(1)} %all-gather.8) | copy-start | bytes 98308
  249.4 4.6 %copy-start.7 = (f32[16,4,128]{2,1,0:T(4,128)}, f32[16,4,128]{2,1,0:T(4,128)S(1)}, u32[]{:S(2)}) copy-start(f32[16,4,128]{2,1,0:T(4,128)S(1)} %all-gather.9) | copy-start | bytes 98308
  249.5 4.5 %slice-start = ((f32[64,128,128]{2,1,0:T(8,128)}), f32[4,128,128]{2,1,0:T(8,128)S(1)}, s32[]{:S(2)}) async-start(f32[64,128,128]{2,1,0:T(8,128)} %all-gather.13.cloned.1.call-done), calls=%async_computation.2 | async-start | bytes 524288 | tf_op jit(solution)/shard_map/slice | solution.py:15
  272.8 5.3 %slice-start.4 = ((f32[16,4,128]{2,1,0:T(4,128)}), f32[15,4,128]{2,1,0:T(4,128)S(1)}, s32[]{:S(2)}) async-start(f32[16,4,128]{2,1,0:T(4,128)} %copy-done.6), calls=%async_computation.6 | async-start | bytes 61440 | tf_op jit(solution)/shard_map/slice | solution.py:16
  272.8 5.3 %slice-start.5 = ((f32[16,4,128]{2,1,0:T(4,128)}), f32[15,4,128]{2,1,0:T(4,128)S(1)}, s32[]{:S(2)}) async-start(f32[16,4,128]{2,1,0:T(4,128)} %copy-done.7), calls=%async_computation.7 | async-start | bytes 61440 | tf_op jit(solution)/shard_map/slice | solution.py:16
  273.6 4.5 %slice-start.1 = ((f32[64,128,128]{2,1,0:T(8,128)}), f32[4,128,128]{2,1,0:T(8,128)S(1)}, s32[]{:S(2)}) async-start(f32[64,128,128]{2,1,0:T(8,128)} %all-gather.15.cloned.1.call-done), calls=%async_computation.3 | async-start | bytes 524288 | tf_op jit(solution)/shard_map/slice | solution.py:15
Sparse Core Ops, SparseCore 0:
  49.2 52.6 all-gather.12
  215.0 34.1 all-gather.14
where the time goes:
time: 306 us; the launch traced here: 304 us
  blocking collectives  163 us (53%)
  local copies, waits for them, and re-layouts  59 us (19%)
  other arithmetic  45.5 us (15%)
  matrix products  16 us (5%)
  between operations  14.5 us (5%)
  starting transfers between devices  5.4 us (2%)
    all_gather x4, blocking collectives, joined(): pieces = jax.tree.map(lambda part: lax.all_gather(part, axis), value)  92.2 us
    all_gather x2, blocking collectives, decode(): queries = lax.all_gather(query, 'tp', axis=1, tiled=True)  71.2 us
    add x30, other arithmetic, join_parts(): one_side[1] * one_scale[:, :, None]  36.2 us
    unnamed x42, local copies, waits for them, and re-layouts  17.5 us
    scatter x3, local copies, waits for them, and re-layouts, migrate(): cache.at[jnp.where(target_slots >= 0, target_slots, slots_here)]  16.6 us
    slice x10, local copies, waits for them, and re-layouts, joined(): tail = jax.tree.map(lambda part: part[1:], pieces)  9.02 us
    gather x2, local copies, waits for them, and re-layouts, migrate(): payload = cache[jnp.maximum(send_rows[:, 0], 0)]  7.06 us
    dot_general x2, matrix products, page_terms(): jnp.einsum('pkgd,pktd->pkgt', picked, cache[:, 0], preferred_element_type...  6.97 us
  transfers between devices with their start and end apart: 6, of which 0 were waited for; matrix products, arithmetic and copies ran while one was open for 24% of the time, Pallas kernels for 0%

commit v1 on v0

v1 whole, which is shorter than its diff:
```python
import functools

import jax
import jax.numpy as jnp
from jax import lax
from jax.experimental import pallas as pl
from jax.experimental.pallas import tpu as pltpu
from jax.sharding import PartitionSpec as P

HEADS = 128
KVH = 8
HD = 128
PAGE = 128
SLOTS = 12
SESS = 4
N_INST = 8
N_TP = 16
MESH = pl.DeviceIdType.MESH
TILES = 32
CHUNK = 2
NCH = TILES // CHUNK
HALF = NCH // 2


def iota(shape, dim):
    return lax.broadcasted_iota(jnp.int32, shape, dim)


def put_row(tile, row, fresh):
    fresh = jnp.broadcast_to(fresh.astype(tile.dtype), tile.shape)
    return jnp.where(iota(tile.shape, 0) == row, fresh, tile)


def exchange_kernel(
    scal, meta, tabs, mine, fresh1, cache,
    out_ref, recv_ref, rmeta_ref,
    cbuf, pay, rel, pages, metas, xmine, xtab, fr2, qall, psend, prec, osc, xsend, xrecv,
    load_sem, m_ss, m_rs, x_ss, x_rs, q_ss, q_rs, p_ss, p_rs, o_ss, o_rs,
    g_ss, g_rs, f_ss, f_rs, r_rs,
):
    i = lax.axis_index("inst")
    t = lax.axis_index("tp")
    xh = i // 4
    y = i % 4

    def inst(h, row):
        return lax.rem(h + 2, 2) * 4 + lax.rem(row + 4, 4)

    def at(k):
        return (lax.rem(i + k + N_INST, N_INST), t)

    def peer(u):
        return lax.rem(t + u, N_TP)

    def remote(src, dst, ss, rs, dev):
        return pltpu.make_async_remote_copy(src, dst, ss, rs, device_id=dev, device_id_type=MESH)

    loads = [pltpu.make_async_copy(cache.at[l], cbuf.at[l], load_sem.at[l]) for l in range(SLOTS)]
    for load in loads:
        load.start()

    barrier = pltpu.get_barrier_semaphore()
    for u in range(1, N_TP):
        pl.semaphore_signal(barrier, 1, device_id=(i, peer(u)), device_id_type=MESH)
    for k in range(1, N_INST):
        pl.semaphore_signal(barrier, 1, device_id=at(k), device_id_type=MESH)
    pl.semaphore_wait(barrier, N_TP + N_INST - 2)

    def meta_copy(u):
        return remote(meta, metas.at[t], m_ss.at[u], m_rs.at[t], (i, peer(u)))

    for u in range(1, N_TP):
        meta_copy(u).start()
    cross = []
    for r in (1, 2):
        cross.append(remote(mine, xmine.at[r - 1], x_ss.at[r - 1], x_rs.at[r - 1], at(-r)))
        cross.append(remote(tabs.at[1], xtab.at[r - 1], x_ss.at[1 + r], x_rs.at[1 + r], at(-r)))
        cross.append(remote(meta, rmeta_ref.at[r - 1], x_ss.at[3 + r], x_rs.at[3 + r], at(r)))
    for copy in cross:
        copy.start()

    for load in loads:
        load.wait()

    def make_pay(r):
        for c in range(2):
            e = (r - 1) * 2 + c
            slot = scal[20 + e]
            row = scal[24 + e]
            sess = scal[28 + e]

            def one(n, carry, slot=slot, row=row, sess=sess, c=c):
                fresh = fresh1[sess, pl.ds(n, 1), :]
                pay[r - 1, c * 16 + n] = put_row(cbuf[slot, n], row, fresh)
                return carry

            lax.fori_loop(0, 16, one, 0)

    def chunk(k):
        return pl.ds(k * CHUNK, CHUNK)

    to_relay = {1: (inst(xh, y + 1), t), 2: (inst(xh, y - 1), t)}

    def direct(r, k):
        return remote(
            pay.at[r - 1, chunk(k)], recv_ref.at[r - 1, chunk(k)],
            g_ss.at[r - 1, k], g_rs.at[r - 1, k], at(r),
        )

    def first_leg(r, k):
        return remote(
            pay.at[r - 1, chunk(k)], rel.at[chunk(k)], g_ss.at[r - 1, k], r_rs.at[k], to_relay[r]
        )

    forward_to = {1: (inst(xh + 1, y), t), 2: (inst(xh + jnp.where(y == 1, 1, 0), y - 1), t)}

    def second_leg(r, k):
        return remote(
            rel.at[chunk(k)], recv_ref.at[r - 1, chunk(k)], f_ss.at[k], g_rs.at[r - 1, k], forward_to[r]
        )

    def each(low, high, fn):
        def body(k, carry):
            fn(k)
            return carry

        lax.fori_loop(low, high, body, 0)

    even = y % 2 == 0
    odd = y % 2 == 1
    last = y == 3
    make_pay(2)

    @pl.when(even)
    def _():
        each(0, HALF, lambda k: first_leg(2, k).start())

    make_pay(1)

    @pl.when(last)
    def _():
        each(0, NCH, lambda k: first_leg(1, k).start())

    @pl.when(y < 3)
    def _():
        each(0, NCH, lambda k: direct(1, k).start())

    @pl.when(odd)
    def _():
        each(0, HALF, lambda k: direct(2, k).start())

    each(HALF, NCH, lambda k: direct(2, k).start())

    def relay_step(k):
        @pl.when(y == 0)
        def _():
            first_leg(1, k).wait_recv()
            second_leg(1, k).start()

    def relay_half(k):
        relay_step(k)

        @pl.when(odd)
        def _():
            first_leg(2, k).wait_recv()
            second_leg(2, k).start()

    for u in range(1, N_TP):
        remote(meta, metas.at[peer(u)], m_ss.at[u], m_rs.at[peer(u)], (i, peer(u))).wait_recv()
    for copy in cross:
        copy.wait_recv()
    codes = meta[...]
    for u in range(1, N_TP):
        codes = jnp.maximum(codes, metas[peer(u)])
    rows8 = iota((8, 128), 0)
    left = []
    arrives = []
    for r in (1, 2):
        a_code = codes[2 * r - 2 : 2 * r - 1, :]
        e_code = codes[2 * r - 1 : 2 * r, :]
        left.append(jnp.minimum(jnp.max(jnp.where(tabs[0] == a_code, rows8, 0)), SESS - 1))
        arrives.append(jnp.minimum(jnp.max(jnp.where(xtab[r - 1] == e_code, rows8, 0)), SESS - 1))

    lower = iota((16, 128), 0) >= 8
    for s in range(SESS):
        own = mine[s].astype(jnp.float32)
        query = own[:16]
        fresh = own[16:]
        for r in (0, 1):
            other = xmine[r, arrives[r]].astype(jnp.float32)
            hit = jnp.where(left[r] == s, 1, 0)
            query = jnp.where(lower & (hit == 1), other[:16], query)
            fresh = jnp.where(hit == 1, other[16:], fresh)
        qall[t, s] = query.astype(jnp.bfloat16)
        fr2[s] = fresh

    def q_copy(u):
        return remote(qall.at[t], qall.at[t], q_ss.at[u], q_rs.at[t], (i, peer(u)))

    for u in range(1, N_TP):
        q_copy(u).start()

    for s in range(SESS):
        for j in range(2):
            e = s * 2 + j
            slot = scal[e]
            row1 = scal[16 + s] - scal[8 + e] * PAGE

            def one(n, carry, slot=slot, row1=row1, s=s, e=e):
                tile = put_row(cbuf[slot, n], row1, fresh1[s, pl.ds(n, 1), :])
                pages[e, n] = put_row(tile, row1 + 1, fr2[s, pl.ds(n, 1), :])
                return carry

            lax.fori_loop(0, 16, one, 0)

    for u in range(1, N_TP):
        remote(
            qall.at[t], qall.at[peer(u)], q_ss.at[u], q_rs.at[peer(u)], (i, peer(u))
        ).wait_recv()

    lane = iota((32, 128), 1)
    step_two = (iota((32, 128), 0) // 8) % 2
    lane_group = lane // 16

    def p_copy(dst):
        return remote(psend.at[dst], prec.at[t], p_ss.at[dst], p_rs.at[t], (i, dst))

    def head_step(kk, carry):
        k = lax.rem(kk + t // 2 + 1, KVH)
        stat = jnp.zeros((32, 128), jnp.float32)
        for s in range(SESS):
            query = qall[pl.ds(2 * k, 2), s].reshape(32, HD)
            tops, totals, sums = [], [], []
            for j in range(2):
                e = s * 2 + j
                scores = lax.dot_general(
                    query, pages[e, k], (((1,), (1,)), ((), ())), preferred_element_type=jnp.float32
                ) * (HD ** -0.5)
                visible = lane + scal[8 + e] * PAGE <= scal[16 + s] + step_two
                top = jnp.max(jnp.where(visible, scores, -1e30), axis=1, keepdims=True)
                weight = jnp.where(visible, jnp.exp(scores - top), 0.0)
                tops.append(top)
                totals.append(jnp.sum(weight, axis=1, keepdims=True))
                sums.append(
                    jnp.dot(
                        weight.astype(jnp.bfloat16), pages[e, KVH + k],
                        preferred_element_type=jnp.float32,
                    )
                )
            top = jnp.maximum(tops[0], tops[1])
            f0 = jnp.exp(tops[0] - top)
            f1 = jnp.exp(tops[1] - top)
            psend[pl.ds(2 * k, 2), s] = (f0 * sums[0] + f1 * sums[1]).reshape(2, 16, HD)
            stat = jnp.where(lane_group == 2 * s, top, stat)
            stat = jnp.where(lane_group == 2 * s + 1, f0 * totals[0] + f1 * totals[1], stat)
        psend[pl.ds(2 * k, 2), SESS] = stat.reshape(2, 16, HD)
        for d in range(2):
            @pl.when(2 * k + d != t)
            def _():
                p_copy(2 * k + d).start()
        relay_half(kk)
        return carry

    lax.fori_loop(0, KVH, head_step, 0)
    each(HALF, HALF + 4, relay_step)

    for u in range(1, N_TP):
        remote(
            psend.at[t], prec.at[peer(u)], p_ss.at[t], p_rs.at[peer(u)], (i, peer(u))
        ).wait_recv()
    prec[t] = psend[t]

    def top_step(u, best):
        return jnp.maximum(best, prec[u, SESS])

    best = lax.fori_loop(1, N_TP, top_step, prec[0, SESS])

    def sum_step(u, carry):
        acc, tot = carry
        stat = prec[u, SESS]
        factor = jnp.exp(stat - best)
        new_acc = []
        new_tot = []
        for s in range(SESS):
            f = factor[:, 32 * s : 32 * s + 1]
            new_acc.append(acc[s] + f * prec[u, s])
            new_tot.append(tot[s] + f * stat[:, 32 * s + 16 : 32 * s + 17])
        return tuple(new_acc), tuple(new_tot)

    zero = jnp.zeros((16, HD), jnp.float32)
    none = jnp.zeros((16, 1), jnp.float32)
    acc, tot = lax.fori_loop(0, N_TP, sum_step, ((zero,) * SESS, (none,) * SESS))
    for s in range(SESS):
        osc[s] = acc[s] / tot[s]

    for r in (0, 1):
        row = osc[left[r]]
        for s in range(SESS):
            xsend[r, s] = jnp.where(arrives[r] == s, row, 0.0).astype(jnp.bfloat16)
    outs = [remote(xsend.at[r], xrecv.at[r], o_ss.at[r], o_rs.at[r], at(r + 1)) for r in (0, 1)]
    for copy in outs:
        copy.start()
    each(HALF + 4, NCH, relay_step)
    for copy in outs:
        copy.wait_recv()
    for s in range(SESS):
        gone = jnp.where((left[0] == s) | (left[1] == s), 1, 0)
        came = xrecv[0, s].astype(jnp.float32) + xrecv[1, s].astype(jnp.float32)
        out_ref[s] = jnp.where(lower & (gone == 1), came, osc[s]).astype(jnp.bfloat16)

    for u in range(1, N_TP):
        meta_copy(u).wait_send()
        q_copy(u).wait_send()
        p_copy(peer(u)).wait_send()
    for copy in cross + outs:
        copy.wait_send()
    for r in (1, 2):
        each(0, NCH, lambda k, r=r: direct(r, k).wait_send())

    @pl.when(y == 0)
    def _():
        each(0, NCH, lambda k: second_leg(1, k).wait_send())

    @pl.when(odd)
    def _():
        each(0, HALF, lambda k: second_leg(2, k).wait_send())

    for r in (1, 2):
        each(0, NCH, lambda k, r=r: direct(r, k).wait_recv())


def exchange(scal, meta, tabs, mine, fresh1, cache):
    vmem = pl.BlockSpec(memory_space=pltpu.VMEM)
    hbm = pl.BlockSpec(memory_space=pl.ANY)
    dma = pltpu.SemaphoreType.DMA
    bf16, f32, i32 = jnp.bfloat16, jnp.float32, jnp.int32
    return pl.pallas_call(
        exchange_kernel,
        name="exchange",
        out_shape=(
            jax.ShapeDtypeStruct((SESS, 16, HD), bf16),
            jax.ShapeDtypeStruct((2, TILES, PAGE, HD), bf16),
            jax.ShapeDtypeStruct((2, 8, 128), i32),
        ),
        in_specs=[pl.BlockSpec(memory_space=pltpu.SMEM), vmem, vmem, vmem, vmem, hbm],
        out_specs=(vmem, hbm, vmem),
        scratch_shapes=[
            pltpu.VMEM((SLOTS, 16, PAGE, HD), bf16),
            pltpu.VMEM((2, TILES, PAGE, HD), bf16),
            pltpu.VMEM((TILES, PAGE, HD), bf16),
            pltpu.VMEM((2 * SESS, 16, PAGE, HD), bf16),
            pltpu.VMEM((N_TP, 8, 128), i32),
            pltpu.VMEM((2, SESS, 32, HD), bf16),
            pltpu.VMEM((2, 8, 128), i32),
            pltpu.VMEM((SESS, 16, HD), f32),
            pltpu.VMEM((N_TP, SESS, 16, HD), bf16),
            pltpu.VMEM((N_TP, SESS + 1, 16, HD), f32),
            pltpu.VMEM((N_TP, SESS + 1, 16, HD), f32),
            pltpu.VMEM((SESS, 16, HD), f32),
            pltpu.VMEM((2, SESS, 16, HD), bf16),
            pltpu.VMEM((2, SESS, 16, HD), bf16),
            dma((SLOTS,)),
            dma((N_TP,)), dma((N_TP,)),
            dma((6,)), dma((6,)),
            dma((N_TP,)), dma((N_TP,)),
            dma((N_TP,)), dma((N_TP,)),
            dma((2,)), dma((2,)),
            dma((2, NCH)), dma((2, NCH)),
            dma((NCH,)), dma((NCH,)),
            dma((NCH,)),
        ],
        compiler_params=pltpu.CompilerParams(
            collective_id=1, has_side_effects=True, vmem_limit_bytes=32 * 1024 * 1024
        ),
    )(scal, meta, tabs, mine, fresh1, cache)


def assemble_kernel(plan, came, fresh, cache, recv, out, buf, in_sem, out_sem):
    targets = [came[r, 4 + 2 * r + c, 0] for r in range(2) for c in range(2)]
    for n, target in enumerate(targets):
        @pl.when(target >= 0)
        def _():
            pltpu.make_async_copy(
                recv.at[n // 2, pl.ds((n % 2) * 16, 16)], buf.at[target], in_sem.at[target]
            ).start()
    for l in range(SLOTS):
        hit = functools.reduce(jnp.logical_or, [target == l for target in targets])

        @pl.when(jnp.logical_not(hit))
        def _():
            pltpu.make_async_copy(cache.at[l], buf.at[l], in_sem.at[l]).start()
    for l in range(SLOTS):
        pltpu.make_async_copy(cache.at[l], buf.at[l], in_sem.at[l]).wait()
    for step in range(2):
        for s in range(SESS):
            slot = plan[step, s]
            row = plan[2 + step, s]

            @pl.when(slot >= 0)
            def _():
                start = pl.multiple_of((row // 16) * 16, 16)

                def one(n, carry):
                    tile = buf[slot, n, pl.ds(start, 16), :]
                    buf[slot, n, pl.ds(start, 16), :] = put_row(
                        tile, row - start, fresh[step, s, pl.ds(n, 1), :]
                    )
                    return carry

                lax.fori_loop(0, 16, one, 0)
    outs = [pltpu.make_async_copy(buf.at[l], out.at[l], out_sem.at[l]) for l in range(SLOTS)]
    for copy in outs:
        copy.start()
    for copy in outs:
        copy.wait()


def assemble(plan, came, fresh, cache, recv):
    vmem = pl.BlockSpec(memory_space=pltpu.VMEM)
    hbm = pl.BlockSpec(memory_space=pl.ANY)
    smem = pl.BlockSpec(memory_space=pltpu.SMEM)
    return pl.pallas_call(
        assemble_kernel,
        name="assemble",
        out_shape=jax.ShapeDtypeStruct(cache.shape, cache.dtype),
        in_specs=[smem, smem, vmem, hbm, hbm],
        out_specs=hbm,
        scratch_shapes=[
            pltpu.VMEM((SLOTS, 16, PAGE, HD), jnp.bfloat16),
            pltpu.SemaphoreType.DMA((SLOTS,)),
            pltpu.SemaphoreType.DMA((SLOTS,)),
        ],
        compiler_params=pltpu.CompilerParams(vmem_limit_bytes=16 * 1024 * 1024),
    )(plan, came, fresh, cache, recv)


def token_place(tables, lengths, tp_index):
    named = jnp.take_along_axis(tables, (lengths // PAGE)[:, None], 1)[:, 0]
    return jnp.where(named // SLOTS == tp_index, named % SLOTS, -1), lengths % PAGE


def shards(
    cache_pool,
    first_query,
    second_query,
    first_fresh,
    second_fresh,
    first_tables,
    second_tables,
    first_lengths,
    second_lengths,
    page_moves,
):
    t = lax.axis_index("tp")
    i = lax.axis_index("inst")
    cache = cache_pool.reshape(SLOTS, 16, PAGE, HD)

    column = jnp.arange(first_tables.shape[1], dtype=jnp.int32)[None, :]
    here = first_tables // SLOTS == t
    number = jnp.stack(
        [
            jnp.min(jnp.where(here, column, first_tables.shape[1] - 1), axis=1),
            jnp.max(jnp.where(here, column, 0), axis=1),
        ],
        axis=1,
    )
    slot = jnp.sum(
        jnp.where(column[:, None, :] == number[:, :, None], first_tables[:, None, :] % SLOTS, 0), axis=2
    )
    moves = jnp.stack(
        [lax.dynamic_index_in_dim(page_moves[0], (i + r) % N_INST, 0, keepdims=False) for r in (1, 2)]
    )
    source, target = moves[..., 0], moves[..., 1]
    pay_slot = jnp.maximum(source, 0).reshape(4)
    mine_of = pay_slot[:, None, None] == slot[None]
    pay_sess = jnp.sum(
        jnp.where(mine_of, jnp.arange(SESS, dtype=jnp.int32)[None, :, None], 0), axis=(1, 2)
    )
    first_row = first_lengths[:, None] - number * PAGE
    pay_row = jnp.sum(jnp.where(mine_of, first_row[None], 0), axis=(1, 2))
    scal = jnp.concatenate(
        [slot.reshape(8), number.reshape(8), first_lengths, pay_slot, pay_row, pay_sess]
    )
    codes = jnp.stack(
        [
            jnp.max(jnp.where(source >= 0, t * SLOTS + source, -1), axis=1),
            jnp.max(jnp.where(target >= 0, t * SLOTS + target, -1), axis=1),
        ],
        axis=1,
    ).reshape(4)
    meta = jnp.broadcast_to(jnp.concatenate([codes, target.reshape(4)])[:, None], (8, 128))
    tabs = jnp.pad(
        jnp.stack([first_tables, second_tables]), ((0, 0), (0, 4), (0, 96)), constant_values=-2
    )
    mine = jnp.concatenate(
        [
            first_query.reshape(SESS, 8, HD),
            second_query.reshape(SESS, 8, HD),
            second_fresh.reshape(SESS, 16, HD),
        ],
        axis=1,
    )
    fresh = jnp.stack([first_fresh.reshape(SESS, 16, HD), second_fresh.reshape(SESS, 16, HD)])
    fresh = fresh.astype(jnp.float32)
    out, recv, came = exchange(scal, meta, tabs, mine, fresh[0], cache)

    slot_one, row_one = token_place(first_tables, first_lengths, t)
    slot_two, row_two = token_place(second_tables, second_lengths, t)
    plan = jnp.stack([slot_one, slot_two, row_one, row_two])
    cache_after = assemble(plan, came, fresh, cache, recv)
    return (
        out[:, :8].reshape(SESS, 8 * HD),
        out[:, 8:].reshape(SESS, 8 * HD),
        cache_after.reshape(cache_pool.shape),
    )


def solution(mesh):
    placed = (
        P(("inst", "tp"), None, None, None, None),
        P("inst", "tp"),
        P("inst", "tp"),
        P("inst", None, None),
        P("inst", None, None),
        P("inst", None),
        P("inst", None),
        P("inst"),
        P("inst"),
        P(("inst", "tp"), None, None, None),
    )
    return jax.shard_map(
        shards,
        mesh=mesh,
        in_specs=placed,
        out_specs=(P("inst", "tp"), P("inst", "tp"), P(("inst", "tp"), None, None, None, None)),
        check_vma=False,
    )
```

time: 306 us -> 88 us (0.29)
  the two profiles are of different devices: /device:TPU:27 before, /device:TPU:1 now
where the time goes in v1:
time: 88 us; the launch traced here: 86.6 us
  Pallas kernels  68.5 us (78%)
  local copies, waits for them, and re-layouts  12.1 us (14%)
  other arithmetic  5.22 us (6%)
    pallas_call x1, Pallas kernels, exchange(): pl.pallas_call(exchange_kernel, name='exchange', out_shape=(jax.ShapeDtyp...  64.3 us
    pallas_call x1, Pallas kernels, assemble(): pl.pallas_call(assemble_kernel, name='assemble', out_shape=jax.ShapeDtype...  4.28 us
    unnamed x5, local copies, waits for them, and re-layouts  3.99 us
    gather x2, local copies, waits for them, and re-layouts, token_place(): named = jnp.take_along_axis(tables, (lengths // PAGE)[:, None], 1)[:, 0]  2.66 us

profile of v1, /device:TPU:1, one launch (start us, length us, event | category | flops | bytes accessed | tf_op | source)
XLA Modules:
  0.0 86.6 jit_solution(4233429319273566146)
XLA Ops:
  0.7 1.0 %dynamic-slice_reduce_fusion.1 = (s32[2,2]{1,0:T(2,128)S(1)}, s32[2,2]{1,0:T(2,128)S(1)}) fusion(s32[1,8,2,2]{1,3,2,0:T(2,128)} %param.21, s32[]{:T(128)S(6)} %select_n.153, s32[]{:T(128)S(6)} %select_n.155), kind=kLoop, calls=%fused_computation.31 | loop fusion | bytes 72 | tf_op jit(solution)/shard_map/jit(dynamic_index_in_dim)/dynamic_slice | solution.py:471
  1.6 0.7 fusion.14
  2.3 0.7 fusion.13
  3.0 1.3 %gather_fusion = s32[4]{0:T(128)S(1)} fusion(s32[4,32]{1,0:T(4,128)} %param.17, s32[4]{0:T(128)S(1)} %or_bitcast_fusion.1), kind=kCustom, calls=%fused_computation.clone | custom fusion | bytes 64 | tf_op jit(solution)/shard_map/jit(take_along_axis)/gather | solution.py:438
  4.3 1.3 %gather_fusion.1 = s32[4]{0:T(128)S(1)} fusion(s32[4,32]{1,0:T(4,128)} %param.18, s32[4]{0:T(128)S(1)} %or_bitcast_fusion), kind=kCustom, calls=%fused_computation.1.clone | custom fusion | bytes 64 | tf_op jit(solution)/shard_map/jit(take_along_axis)/gather | solution.py:438
  5.7 0.7 compare_select_fusion.6
  6.4 0.3 fusion.3
  6.7 0.1 reshape_squeeze.3
  6.8 0.2 fusion.2
  6.9 0.1 copy.23
  7.0 0.1 reshape.252
  7.1 0.1 pad_add_fusion.7
  7.2 0.1 max.12
  7.3 0.8 select_reduce_fusion.2
  8.1 0.7 multiply_subtract_fusion
  8.8 0.2 select_reduce_fusion
  9.0 0.2 fusion.1
  9.2 0.1 copy.21
  9.3 0.1 reshape.250
  9.4 0.1 copy.22
  9.5 0.1 reshape.251
  9.5 0.7 concatenate.13.scal
  10.3 0.1 broadcast_in_dim.88.meta
  10.4 0.7 pad_add_fusion
  11.1 0.7 stack_reshape.6
  11.8 0.7 stack_reshape.7
  12.5 0.7 reshape.255
  13.3 0.7 copy_bitcast_fusion.2
  14.0 0.0 copy-start
  14.0 2.8 %copy-done = bf16[12,2,8,128,128]{4,3,2,1,0:T(8,128)(2,1)S(1)} copy-done((bf16[12,2,8,128,128]{4,3,2,1,0:T(8,128)(2,1)S(1)}, bf16[12,2,8,128,128]{4,3,2,1,0:T(8,128)(2,1)}, u32[]{:S(2)}) %copy-start) | copy-done | bytes 6291480
  16.8 64.3 %exchange.1 = (bf16[4,16,128]{2,1,0:T(8,128)(2,1)S(1)}, bf16[2,32,128,128]{3,2,1,0:T(8,128)(2,1)S(1)}, s32[2,8,128]{2,1,0:T(8,128)S(1)}) custom-call(s32[32]{0:T(128)S(1)} %concatenate.13.scal, s32[8,128]{1,0:T(8,128)S(1)} %broadcast_in_dim.88.meta, s32[2,8,128]{2,1,0:T(8,128)S(1)} %pad.4.tabs, bf16[4,32,128]{2,1,0:T(8,128)(2,1)S(1)} %pad_maximum_fusion.mine, ...), custom_call_target="tpu_custom_call" | custom-call | tf_op jit(solution)/shard_map/exchange/pallas_call | solution.py:337
  81.1 0.6 copy.32
  81.7 0.6 copy.33
  82.3 4.3 %assemble.1 = bf16[12,16,128,128]{3,2,1,0:T(8,128)(2,1)} custom-call(s32[4,4]{1,0:T(4,128)S(1)} %pad_add_fusion.2.plan, s32[2,8,128]{2,1,0:T(8,128)S(1)} %get-tuple-element.8.came, f32[2,4,16,128]{3,2,1,0:T(8,128)S(1)} %maximum_convert_fusion.fresh, bf16[12,16,128,128]{3,2,1,0:T(8,128)(2,1)S(1)} %bitcast.89, bf16[2,32,128,128]{3,2,1,0:T(8,128)(2,1)S(1)} %get-tuple-element.9.recv), custom_call_target="tpu_custom_call" | custom-call | tf_op jit(solution)/shard_map/assemble/pallas_call | solution.py:422
  (12 shorter events, 0.1 us)
Async XLA Ops:
  14.0 2.8 %copy-start = (bf16[12,2,8,128,128]{4,3,2,1,0:T(8,128)(2,1)S(1)}, bf16[12,2,8,128,128]{4,3,2,1,0:T(8,128)(2,1)}, u32[]{:S(2)}) copy-start(bf16[12,2,8,128,128]{4,3,2,1,0:T(8,128)(2,1)} %param.12) | copy-start | bytes 18874372

commit v2 on v1

v2 whole, which is shorter than its diff:
```python
import functools

import jax
import jax.numpy as jnp
from jax import lax
from jax.experimental import pallas as pl
from jax.experimental.pallas import tpu as pltpu
from jax.sharding import PartitionSpec as P

HEADS = 128
KVH = 8
HD = 128
PAGE = 128
SLOTS = 12
SESS = 4
N_INST = 8
N_TP = 16
MESH = pl.DeviceIdType.MESH
TILES = 32
CHUNK = 2
NCH = TILES // CHUNK
HALF = NCH // 2
BIG = 8
NBIG = TILES // BIG


def iota(shape, dim):
    return lax.broadcasted_iota(jnp.int32, shape, dim)


def one_hot(row):
    hot = jnp.where(iota((PAGE, HD), 0) == row, 1.0, 0.0).astype(jnp.bfloat16)
    return hot.reshape(8, 16, HD)


def spread(row):
    return jnp.broadcast_to(row, (16, HD)).astype(jnp.bfloat16)[None]


def heads_apart(flat, into, row):
    for h in range(KVH):
        into[:, row + h, :] = flat[:, h * HD : (h + 1) * HD].astype(into.dtype)


def exchange_kernel(
    ft, n1, moves, first_tab, second_tab, first_query, second_query, first_fresh, second_fresh, cache,
    out_ref, recv_ref, rmeta_ref,
    cbuf, pay, rel, pages, meta, metas, mytab, xtab, mine32, fr1, mine, xmine, fr2, qall, psend, prec,
    osc, xsend, xrecv,
    load_sem, m_ss, m_rs, x_ss, x_rs, q_ss, q_rs, p_ss, p_rs, o_ss, o_rs,
    g_ss, g_rs, f_ss, f_rs, r_rs,
):
    i = lax.axis_index("inst")
    t = lax.axis_index("tp")
    xh = i // 4
    y = i % 4

    def inst(h, row):
        return lax.rem(h + 2, 2) * 4 + lax.rem(row + 4, 4)

    def at(k):
        return (lax.rem(i + k + N_INST, N_INST), t)

    def peer(u):
        return lax.rem(t + u, N_TP)

    def remote(src, dst, ss, rs, dev):
        return pltpu.make_async_remote_copy(src, dst, ss, rs, device_id=dev, device_id_type=MESH)

    loads = [pltpu.make_async_copy(cache.at[l], cbuf.at[l], load_sem.at[l]) for l in range(SLOTS)]
    for load in loads:
        load.start()

    barrier = pltpu.get_barrier_semaphore()
    for u in range(1, N_TP):
        pl.semaphore_signal(barrier, 1, device_id=(i, peer(u)), device_id_type=MESH)
    for k in range(1, N_INST):
        pl.semaphore_signal(barrier, 1, device_id=at(k), device_id_type=MESH)

    low = t * SLOTS
    slots, numbers = [], []
    for s in range(SESS):
        def look(p, found, s=s):
            slot0, slot1, page0, page1 = found
            v = ft[s, p] - low
            hit = (v >= 0) & (v < SLOTS)
            new = hit & (page0 < 0)
            return (
                jnp.where(new, v, slot0), jnp.where(hit, v, slot1),
                jnp.where(new, p, page0), jnp.where(hit, p, page1),
            )

        zero, none = jnp.int32(0), jnp.int32(-1)
        slot0, slot1, page0, page1 = lax.fori_loop(0, 32, look, (zero, zero, none, none), unroll=8)
        slots += [slot0, slot1]
        numbers += [page0, page1]

    rows8 = iota((8, 128), 0)
    sources, targets = {}, {}
    table = jnp.zeros((8, 128), jnp.int32)
    for r in (1, 2):
        b = lax.rem(i + r, N_INST)
        a_code = e_code = jnp.int32(-1)
        for c in range(2):
            a, e = moves[0, b, c, 0], moves[0, b, c, 1]
            sources[r, c] = a
            a_code = jnp.maximum(a_code, jnp.where(a >= 0, low + a, -1))
            e_code = jnp.maximum(e_code, jnp.where(e >= 0, low + e, -1))
            table = jnp.where(rows8 == 4 + 2 * (r - 1) + c, e, table)
        table = jnp.where(rows8 == 2 * r - 2, a_code, table)
        table = jnp.where(rows8 == 2 * r - 1, e_code, table)
    meta[...] = table
    mytab[...] = jnp.full((8, 128), -2, jnp.int32)
    mytab[0:SESS, 0:32] = second_tab[...]
    heads_apart(first_query[...].astype(jnp.float32), mine32, 0)
    heads_apart(second_query[...].astype(jnp.float32), mine32, 8)
    for s in range(SESS):
        token = first_fresh[s].astype(jnp.float32)
        other = second_fresh[s].astype(jnp.float32)
        for h in range(KVH):
            fr1[s, :, h, :] = token[:, h * HD : (h + 1) * HD]
            for kv in range(2):
                mine32[s, 16 + kv * 8 + h, :] = other[kv, h * HD : (h + 1) * HD]
    for s in range(SESS):
        mine[s] = mine32[s].astype(jnp.bfloat16)

    for load in loads:
        load.wait()

    def make_pay(r):
        for c in range(2):
            slot = jnp.maximum(sources[r, c], 0)
            sess = row = jnp.int32(0)
            for e in range(2 * SESS):
                mine_is = slots[e] == slot
                sess = jnp.where(mine_is, e // 2, sess)
                row = jnp.where(mine_is, n1[e // 2] - numbers[e] * PAGE, row)
            hot = one_hot(row)
            keep = 1 - hot

            def one(n, carry, slot=slot, sess=sess, hot=hot, keep=keep, c=c):
                fresh = spread(fr1[sess, n // 8, pl.ds(n % 8, 1), :])
                tile = cbuf[slot, n].reshape(8, 16, HD) * keep + fresh * hot
                pay[r - 1, c * 16 + n] = tile.reshape(PAGE, HD)
                return carry

            lax.fori_loop(0, 16, one, 0, unroll=4)

    make_pay(1)
    make_pay(2)
    pl.semaphore_wait(barrier, N_TP + N_INST - 2)

    def meta_copy(u):
        return remote(meta, metas.at[t], m_ss.at[u], m_rs.at[t], (i, peer(u)))

    for u in range(1, N_TP):
        meta_copy(u).start()
    cross = []
    for r in (1, 2):
        cross.append(remote(mine, xmine.at[r - 1], x_ss.at[r - 1], x_rs.at[r - 1], at(-r)))
        cross.append(remote(mytab, xtab.at[r - 1], x_ss.at[1 + r], x_rs.at[1 + r], at(-r)))
        cross.append(remote(meta, rmeta_ref.at[r - 1], x_ss.at[3 + r], x_rs.at[3 + r], at(r)))
    for copy in cross:
        copy.start()

    def chunk(k):
        return pl.ds(k * CHUNK, CHUNK)

    to_relay = {1: (inst(xh, y + 1), t), 2: (inst(xh, y - 1), t)}

    def direct(r, q):
        tiles = pl.ds(q * BIG, BIG)
        return remote(
            pay.at[r - 1, tiles], recv_ref.at[r - 1, tiles],
            g_ss.at[r - 1, NCH + q], g_rs.at[r - 1, NCH + q], at(r),
        )

    def first_leg(r, k):
        return remote(
            pay.at[r - 1, chunk(k)], rel.at[chunk(k)], g_ss.at[r - 1, k], r_rs.at[k], to_relay[r]
        )

    forward_to = {1: (inst(xh + 1, y), t), 2: (inst(xh + jnp.where(y == 1, 1, 0), y - 1), t)}

    def second_leg(r, k):
        return remote(
            rel.at[chunk(k)], recv_ref.at[r - 1, chunk(k)], f_ss.at[k], g_rs.at[r - 1, k], forward_to[r]
        )

    def each(low, high, fn):
        def body(k, carry):
            fn(k)
            return carry

        lax.fori_loop(low, high, body, 0)

    even = y % 2 == 0
    odd = y % 2 == 1
    last = y == 3
    @pl.when(even)
    def _():
        each(0, HALF, lambda k: first_leg(2, k).start())

    @pl.when(last)
    def _():
        each(0, NCH, lambda k: first_leg(1, k).start())

    @pl.when(y < 3)
    def _():
        each(0, NBIG, lambda q: direct(1, q).start())

    def relay_one(low, high):
        @pl.when(y == 0)
        def _():
            def step(k):
                first_leg(1, k).wait_recv()
                second_leg(1, k).start()

            each(low, high, step)

    def relay_two(low, high):
        @pl.when(odd)
        def _():
            def step(k):
                first_leg(2, k).wait_recv()
                second_leg(2, k).start()

            each(low, high, step)

    for u in range(1, N_TP):
        remote(meta, metas.at[peer(u)], m_ss.at[u], m_rs.at[peer(u)], (i, peer(u))).wait_recv()
    for copy in cross:
        copy.wait_recv()
    codes = meta[...]
    for u in range(1, N_TP):
        codes = jnp.maximum(codes, metas[peer(u)])
    left = []
    arrives = []
    for r in (1, 2):
        a_code = codes[2 * r - 2 : 2 * r - 1, :]
        e_code = codes[2 * r - 1 : 2 * r, :]
        left.append(jnp.minimum(jnp.max(jnp.where(first_tab[...] == a_code[:, :32], rows8[:SESS, :32], 0)), SESS - 1))
        arrives.append(jnp.minimum(jnp.max(jnp.where(xtab[r - 1] == e_code, rows8, 0)), SESS - 1))

    relay_two(0, 2)
    relay_one(0, 2)

    lower = iota((16, 128), 0) >= 8
    for s in range(SESS):
        own = mine[s].astype(jnp.float32)
        query = own[:16]
        fresh = own[16:]
        for r in (0, 1):
            other = xmine[r, arrives[r]].astype(jnp.float32)
            hit = jnp.where(left[r] == s, 1, 0)
            query = jnp.where(lower & (hit == 1), other[:16], query)
            fresh = jnp.where(hit == 1, other[16:], fresh)
        qall[t, s] = query.astype(jnp.bfloat16)
        fr2[s] = fresh

    def q_copy(u):
        return remote(qall.at[t], qall.at[t], q_ss.at[u], q_rs.at[t], (i, peer(u)))

    for u in range(1, N_TP):
        q_copy(u).start()

    for s in range(SESS):
        for j in range(2):
            e = s * 2 + j
            slot = slots[e]
            row1 = n1[s] - numbers[e] * PAGE
            hot1 = one_hot(row1)
            hot2 = one_hot(row1 + 1)
            keep = 1 - hot1 - hot2

            def one(n, carry, slot=slot, hot1=hot1, hot2=hot2, keep=keep, s=s, e=e):
                fresh1 = spread(fr1[s, n // 8, pl.ds(n % 8, 1), :])
                fresh2 = spread(fr2[s, pl.ds(n, 1), :])
                tile = cbuf[slot, n].reshape(8, 16, HD) * keep + fresh1 * hot1 + fresh2 * hot2
                pages[e, n] = tile.reshape(PAGE, HD)
                return carry

            lax.fori_loop(0, 16, one, 0, unroll=4)

    relay_two(2, 4)
    relay_one(2, 3)
    for u in range(1, N_TP):
        remote(
            qall.at[t], qall.at[peer(u)], q_ss.at[u], q_rs.at[peer(u)], (i, peer(u))
        ).wait_recv()

    relay_two(4, HALF)

    @pl.when(odd)
    def _():
        each(0, NBIG, lambda q: direct(2, q).start())

    relay_one(3, 6)

    lane = iota((32, 128), 1)
    step_two = (iota((32, 128), 0) // 8) % 2
    lane_group = lane // 16

    def p_copy(dst):
        return remote(psend.at[dst], prec.at[t], p_ss.at[dst], p_rs.at[t], (i, dst))

    def head_step(kk, carry):
        k = lax.rem(kk + t // 2 + 1, KVH)
        stat = jnp.zeros((32, 128), jnp.float32)
        for s in range(SESS):
            query = qall[pl.ds(2 * k, 2), s].reshape(32, HD)
            keys = pages[pl.ds(2 * s, 2), k].reshape(2 * PAGE, HD)
            both = lax.dot_general(
                query, keys, (((1,), (1,)), ((), ())), preferred_element_type=jnp.float32
            ) * (HD ** -0.5)
            tops, totals, sums = [], [], []
            for j in range(2):
                e = s * 2 + j
                scores = both[:, j * PAGE : (j + 1) * PAGE]
                visible = lane + numbers[e] * PAGE <= n1[s] + step_two
                top = jnp.max(jnp.where(visible, scores, -1e30), axis=1, keepdims=True)
                weight = jnp.where(visible, jnp.exp(scores - top), 0.0)
                tops.append(top)
                totals.append(jnp.sum(weight, axis=1, keepdims=True))
                sums.append(
                    jnp.dot(
                        weight.astype(jnp.bfloat16), pages[e, KVH + k],
                        preferred_element_type=jnp.float32,
                    )
                )
            top = jnp.maximum(tops[0], tops[1])
            f0 = jnp.exp(tops[0] - top)
            f1 = jnp.exp(tops[1] - top)
            psend[pl.ds(2 * k, 2), s] = (f0 * sums[0] + f1 * sums[1]).reshape(2, 16, HD)
            stat = jnp.where(lane_group == 2 * s, top, stat)
            stat = jnp.where(lane_group == 2 * s + 1, f0 * totals[0] + f1 * totals[1], stat)
        psend[pl.ds(2 * k, 2), SESS] = stat.reshape(2, 16, HD)
        for d in range(2):
            @pl.when(2 * k + d != t)
            def _():
                p_copy(2 * k + d).start()
        relay_one(kk + 6, kk + 7)
        return carry

    lax.fori_loop(0, KVH, head_step, 0)
    relay_one(NCH - 2, NCH)

    @pl.when(last)
    def _():
        each(0, NCH, lambda k: first_leg(1, k).wait_send())

    @pl.when(y < 3)
    def _():
        each(0, NBIG, lambda q: direct(1, q).wait_send())

    @pl.when(even)
    def _():
        each(NBIG // 2, NBIG, lambda q: direct(2, q).start())

    for u in range(1, N_TP):
        remote(
            psend.at[t], prec.at[peer(u)], p_ss.at[t], p_rs.at[peer(u)], (i, peer(u))
        ).wait_recv()
    prec[t] = psend[t]
    def top_step(u, best):
        return jnp.maximum(best, prec[u, SESS])

    best = lax.fori_loop(1, N_TP, top_step, prec[0, SESS])

    def sum_step(u, carry):
        acc, tot = carry
        stat = prec[u, SESS]
        factor = jnp.exp(stat - best)
        new_acc = []
        new_tot = []
        for s in range(SESS):
            f = factor[:, 32 * s : 32 * s + 1]
            new_acc.append(acc[s] + f * prec[u, s])
            new_tot.append(tot[s] + f * stat[:, 32 * s + 16 : 32 * s + 17])
        return tuple(new_acc), tuple(new_tot)

    zero = jnp.zeros((16, HD), jnp.float32)
    none = jnp.zeros((16, 1), jnp.float32)
    acc, tot = lax.fori_loop(0, N_TP, sum_step, ((zero,) * SESS, (none,) * SESS))
    for s in range(SESS):
        osc[s] = acc[s] / tot[s]

    for r in (0, 1):
        row = osc[left[r]]
        for s in range(SESS):
            xsend[r, s] = jnp.where(arrives[r] == s, row, 0.0).astype(jnp.bfloat16)
    outs = [remote(xsend.at[r], xrecv.at[r], o_ss.at[r], o_rs.at[r], at(r + 1)) for r in (0, 1)]
    for copy in outs:
        copy.start()
    for copy in outs:
        copy.wait_recv()
    for s in range(SESS):
        gone = jnp.where((left[0] == s) | (left[1] == s), 1, 0)
        came = xrecv[0, s].astype(jnp.float32) + xrecv[1, s].astype(jnp.float32)
        out_ref[s] = jnp.where(lower & (gone == 1), came, osc[s])

    for u in range(1, N_TP):
        meta_copy(u).wait_send()
        q_copy(u).wait_send()
        p_copy(peer(u)).wait_send()
    for copy in cross + outs:
        copy.wait_send()
    @pl.when(y == 0)
    def _():
        each(0, NCH, lambda k: second_leg(1, k).wait_send())

    @pl.when(odd)
    def _():
        each(0, HALF, lambda k: second_leg(2, k).wait_send())
        each(0, NBIG, lambda q: direct(2, q).wait_send())

    @pl.when(even)
    def _():
        each(0, HALF, lambda k: first_leg(2, k).wait_send())
        each(NBIG // 2, NBIG, lambda q: direct(2, q).wait_send())

    @pl.when(y == 0)
    def _():
        each(0, NCH, lambda k: second_leg(1, k).wait_recv())

    @pl.when(y > 0)
    def _():
        each(0, NBIG, lambda q: direct(1, q).wait_recv())

    @pl.when(odd)
    def _():
        each(0, NBIG, lambda q: direct(2, q).wait_recv())

    @pl.when(even)
    def _():
        each(0, HALF, lambda k: second_leg(2, k).wait_recv())
        each(NBIG // 2, NBIG, lambda q: direct(2, q).wait_recv())


def exchange(ft, n1, moves, st, first_query, second_query, first_fresh, second_fresh, cache):
    vmem = pl.BlockSpec(memory_space=pltpu.VMEM)
    smem = pl.BlockSpec(memory_space=pltpu.SMEM)
    hbm = pl.BlockSpec(memory_space=pl.ANY)
    dma = pltpu.SemaphoreType.DMA
    bf16, f32, i32 = jnp.bfloat16, jnp.float32, jnp.int32
    return pl.pallas_call(
        exchange_kernel,
        name="exchange",
        out_shape=(
            jax.ShapeDtypeStruct((SESS, 16, HD), f32),
            jax.ShapeDtypeStruct((2, TILES, PAGE, HD), bf16),
            jax.ShapeDtypeStruct((2, 8, 128), i32),
        ),
        in_specs=[smem, smem, smem] + [vmem] * 6 + [hbm],
        out_specs=(vmem, hbm, vmem),
        scratch_shapes=[
            pltpu.VMEM((SLOTS, 16, PAGE, HD), bf16),
            pltpu.VMEM((2, TILES, PAGE, HD), bf16),
            pltpu.VMEM((TILES, PAGE, HD), bf16),
            pltpu.VMEM((2 * SESS, 16, PAGE, HD), bf16),
            pltpu.VMEM((8, 128), i32),
            pltpu.VMEM((N_TP, 8, 128), i32),
            pltpu.VMEM((8, 128), i32),
            pltpu.VMEM((2, 8, 128), i32),
            pltpu.VMEM((SESS, 32, HD), f32),
            pltpu.VMEM((SESS, 2, 8, HD), f32),
            pltpu.VMEM((SESS, 32, HD), bf16),
            pltpu.VMEM((2, SESS, 32, HD), bf16),
            pltpu.VMEM((SESS, 16, HD), f32),
            pltpu.VMEM((N_TP, SESS, 16, HD), bf16),
            pltpu.VMEM((N_TP, SESS + 1, 16, HD), f32),
            pltpu.VMEM((N_TP, SESS + 1, 16, HD), f32),
            pltpu.VMEM((SESS, 16, HD), f32),
            pltpu.VMEM((2, SESS, 16, HD), bf16),
            pltpu.VMEM((2, SESS, 16, HD), bf16),
            dma((SLOTS,)),
            dma((N_TP,)), dma((N_TP,)),
            dma((6,)), dma((6,)),
            dma((N_TP,)), dma((N_TP,)),
            dma((N_TP,)), dma((N_TP,)),
            dma((2,)), dma((2,)),
            dma((2, NCH + NBIG)), dma((2, NCH + NBIG)),
            dma((NCH,)), dma((NCH,)),
            dma((NCH,)),
        ],
        compiler_params=pltpu.CompilerParams(
            collective_id=1, has_side_effects=True, vmem_limit_bytes=56 * 1024 * 1024
        ),
    )(ft, n1, moves, ft, st, first_query, second_query, first_fresh, second_fresh, cache)


def assemble_kernel(
    came, ft, st, n1, n2, fresh1, fresh2, rows, cache, recv, first_out, second_out, out,
    buf, in_sem, out_sem,
):
    low = lax.axis_index("tp") * SLOTS
    targets = [came[r, 4 + 2 * r + c, 0] for r in range(2) for c in range(2)]
    for n, target in enumerate(targets):
        @pl.when(target >= 0)
        def _():
            pltpu.make_async_copy(
                recv.at[n // 2, pl.ds((n % 2) * 16, 16)], buf.at[target], in_sem.at[target]
            ).start()
    for l in range(SLOTS):
        hit = functools.reduce(jnp.logical_or, [target == l for target in targets])

        @pl.when(jnp.logical_not(hit))
        def _():
            pltpu.make_async_copy(cache.at[l], buf.at[l], in_sem.at[l]).start()
    for h in range(KVH):
        first_out[:, h * HD : (h + 1) * HD] = rows[:, h, :].astype(first_out.dtype)
        second_out[:, h * HD : (h + 1) * HD] = rows[:, 8 + h, :].astype(second_out.dtype)
    for l in range(SLOTS):
        pltpu.make_async_copy(cache.at[l], buf.at[l], in_sem.at[l]).wait()
    for tables, lengths, fresh in ((ft, n1, fresh1), (st, n2, fresh2)):
        for s in range(SESS):
            slot = tables[s, lengths[s] // PAGE] - low
            row = lengths[s] % PAGE

            @pl.when((slot >= 0) & (slot < SLOTS))
            def _():
                start = pl.multiple_of((row // 16) * 16, 16)
                put = iota((16, HD), 0) == row - start
                token = fresh[s].astype(jnp.float32)
                for n in range(16):
                    new = token[n // 8 : n // 8 + 1, (n % 8) * HD : (n % 8 + 1) * HD]
                    tile = buf[slot, n, pl.ds(start, 16), :].astype(jnp.float32)
                    buf[slot, n, pl.ds(start, 16), :] = jnp.where(put, new, tile).astype(jnp.bfloat16)
    outs = [pltpu.make_async_copy(buf.at[l], out.at[l], out_sem.at[l]) for l in range(SLOTS)]
    for copy in outs:
        copy.start()
    for copy in outs:
        copy.wait()


def assemble(came, ft, st, n1, n2, fresh1, fresh2, rows, cache, recv):
    vmem = pl.BlockSpec(memory_space=pltpu.VMEM)
    hbm = pl.BlockSpec(memory_space=pl.ANY)
    smem = pl.BlockSpec(memory_space=pltpu.SMEM)
    flat = jax.ShapeDtypeStruct((SESS, 8 * HD), jnp.bfloat16)
    return pl.pallas_call(
        assemble_kernel,
        name="assemble",
        out_shape=(flat, flat, jax.ShapeDtypeStruct(cache.shape, cache.dtype)),
        in_specs=[smem] * 5 + [vmem] * 3 + [hbm] * 2,
        out_specs=(vmem, vmem, hbm),
        scratch_shapes=[
            pltpu.VMEM((SLOTS, 16, PAGE, HD), jnp.bfloat16),
            pltpu.SemaphoreType.DMA((SLOTS,)),
            pltpu.SemaphoreType.DMA((SLOTS,)),
        ],
        compiler_params=pltpu.CompilerParams(vmem_limit_bytes=56 * 1024 * 1024),
    )(came, ft, st, n1, n2, fresh1, fresh2, rows, cache, recv)


def shards(
    cache_pool,
    first_query,
    second_query,
    first_fresh,
    second_fresh,
    first_tables,
    second_tables,
    first_lengths,
    second_lengths,
    page_moves,
):
    cache = cache_pool.reshape(SLOTS, 16, PAGE, HD)
    rows, recv, came = exchange(
        first_tables, first_lengths, page_moves, second_tables, first_query, second_query,
        first_fresh, second_fresh, cache,
    )
    first_out, second_out, cache_after = assemble(
        came, first_tables, second_tables, first_lengths, second_lengths, first_fresh, second_fresh,
        rows, cache, recv,
    )
    return first_out, second_out, cache_after.reshape(cache_pool.shape)


def solution(mesh):
    placed = (
        P(("inst", "tp"), None, None, None, None),
        P("inst", "tp"),
        P("inst", "tp"),
        P("inst", None, None),
        P("inst", None, None),
        P("inst", None),
        P("inst", None),
        P("inst"),
        P("inst"),
        P(("inst", "tp"), None, None, None),
    )
    return jax.shard_map(
        shards,
        mesh=mesh,
        in_specs=placed,
        out_specs=(P("inst", "tp"), P("inst", "tp"), P(("inst", "tp"), None, None, None, None)),
        check_vma=False,
    )
```

time: 88 us -> 73.2 us (0.83); the launches traced: 86.6 us -> 72.9 us
  local copies, waits for them, and re-layouts: 12.1 us -> 1.36 us
  other arithmetic: 5.22 us -> 0 us
  Pallas kernels: 68.5 us -> 70.9 us
    pallas_call x1, Pallas kernels: 4.28 us -> 7.26 us  [assemble(): pl.pallas_call(assemble_kernel, name='assemble', out_shape=(flat, flat, j...]
    gather x2 -> x0, local copies, waits for them, and re-layouts: 2.66 us -> none  [token_place(): named = jnp.take_along_axis(tables, (lengths // PAGE)[:, None], 1)[:, 0]]
    unnamed x5 -> x1, local copies, waits for them, and re-layouts: 3.99 us -> 1.36 us
    another operation x6 -> x0, local copies, waits for them, and re-layouts: 1.74 us -> none  [the longest x2 1.47 us: shards(): jnp.stack([first_fresh.reshape(SESS, 16, HD), second_fresh.reshape(SESS,...]
    reshape x5 -> x0, local copies, waits for them, and re-layouts: 1.71 us -> none  [the longest x1 0.74 us: shards(): second_fresh.reshape(SESS, 16, HD)]
    reshape x2 -> x0, other arithmetic: 1.34 us -> none  [token_place(): named = jnp.take_along_axis(tables, (lengths // PAGE)[:, None], 1)[:, 0]]
    dynamic_slice x1 -> x0, local copies, waits for them, and re-layouts: 0.97 us -> none  [shards(): lax.dynamic_index_in_dim(page_moves[0], (i + r) % N_INST, 0, keepdims=False)]
where the time goes in v2:
time: 73.2 us; the launch traced here: 72.9 us
  Pallas kernels  70.9 us (97%)
  local copies, waits for them, and re-layouts  1.36 us (2%)
    pallas_call x1, Pallas kernels, exchange(): pl.pallas_call(exchange_kernel, name='exchange', out_shape=(jax.ShapeDtyp...  63.6 us
    pallas_call x1, Pallas kernels, assemble(): pl.pallas_call(assemble_kernel, name='assemble', out_shape=(flat, flat, j...  7.26 us

profile of v2, /device:TPU:1, one launch (start us, length us, event | category | flops | bytes accessed | tf_op | source)
XLA Modules:
  0.0 72.9 jit_solution(11704512222940661913)
XLA Ops:
  0.6 1.4 %copy.13.moves = s32[1,8,2,2]{3,2,1,0:T(2,128)} copy(s32[1,8,2,2]{1,3,2,0:T(2,128)} %param.19) | data formatting | bytes 256 | tf_op args[9]
  2.0 63.6 %exchange.1 = (f32[4,16,128]{2,1,0:T(8,128)}, bf16[2,32,128,128]{3,2,1,0:T(8,128)(2,1)}, s32[2,8,128]{2,1,0:T(8,128)}) custom-call(s32[4,32]{1,0:T(4,128)} %ft.3, s32[4]{0:T(128)} %n1.3, s32[1,8,2,2]{3,2,1,0:T(2,128)} %copy.13.moves, s32[4,32]{1,0:T(4,128)} %ft.3, s32[4,32]{1,0:T(4,128)} %st.1, bf16[4,1024]{1,0:T(4,128)(2,1)} %first_query.1, ...), custom_call_target="tpu_custom_call" | custom-call | tf_op jit(solution)/shard_map/exchange/pallas_call | solution.py:446
  65.6 7.3 %assemble.1 = (bf16[4,1024]{1,0:T(4,128)(2,1)}, bf16[4,1024]{1,0:T(4,128)(2,1)}, bf16[12,16,128,128]{3,2,1,0:T(8,128)(2,1)}) custom-call(s32[2,8,128]{2,1,0:T(8,128)} %get-tuple-element.9.came, s32[4,32]{1,0:T(4,128)} %ft.3, s32[4,32]{1,0:T(4,128)} %st.1, s32[4]{0:T(128)} %n1.3, s32[4]{0:T(128)} %n2.1, bf16[4,2,1024]{2,1,0:T(2,128)(2,1)} %fresh1.1, ...), custom_call_target="tpu_custom_call" | custom-call | tf_op jit(solution)/shard_map/assemble/pallas_call | solution.py:541

commit v3 on v2

--- a/solution.py
+++ b/solution.py
@@ -37,15 +37,10 @@
     return jnp.broadcast_to(row, (16, HD)).astype(jnp.bfloat16)[None]
 
 
-def heads_apart(flat, into, row):
-    for h in range(KVH):
-        into[:, row + h, :] = flat[:, h * HD : (h + 1) * HD].astype(into.dtype)
-
-
 def exchange_kernel(
-    ft, n1, moves, first_tab, second_tab, first_query, second_query, first_fresh, second_fresh, cache,
-    out_ref, recv_ref, rmeta_ref,
-    cbuf, pay, rel, pages, meta, metas, mytab, xtab, mine32, fr1, mine, xmine, fr2, qall, psend, prec,
+    ints, moves, tabs, queries, tokens, cache,
+    out_ref, recv_ref, rmeta_ref, cbuf,
+    pay, rel, pages, meta, metas, xtab, mine32, fr1, mine, xmine, fr2, qall, psend, prec,
     osc, xsend, xrecv,
     load_sem, m_ss, m_rs, x_ss, x_rs, q_ss, q_rs, p_ss, p_rs, o_ss, o_rs,
     g_ss, g_rs, f_ss, f_rs, r_rs,
@@ -78,11 +73,13 @@
         pl.semaphore_signal(barrier, 1, device_id=at(k), device_id_type=MESH)
 
     low = t * SLOTS
+    n1 = [ints[16, s] for s in range(SESS)]
+    n2 = [ints[24, s] for s in range(SESS)]
     slots, numbers = [], []
     for s in range(SESS):
         def look(p, found, s=s):
             slot0, slot1, page0, page1 = found
-            v = ft[s, p] - low
+            v = ints[s, p] - low
             hit = (v >= 0) & (v < SLOTS)
             new = hit & (page0 < 0)
             return (
@@ -101,8 +98,9 @@
     for r in (1, 2):
         b = lax.rem(i + r, N_INST)
         a_code = e_code = jnp.int32(-1)
+        pairs = moves[0, b]
         for c in range(2):
-            a, e = moves[0, b, c, 0], moves[0, b, c, 1]
+            a, e = pairs[c, 0], pairs[c, 1]
             sources[r, c] = a
             a_code = jnp.maximum(a_code, jnp.where(a >= 0, low + a, -1))
             e_code = jnp.maximum(e_code, jnp.where(e >= 0, low + e, -1))
@@ -110,17 +108,17 @@
         table = jnp.where(rows8 == 2 * r - 2, a_code, table)
         table = jnp.where(rows8 == 2 * r - 1, e_code, table)
     meta[...] = table
-    mytab[...] = jnp.full((8, 128), -2, jnp.int32)
-    mytab[0:SESS, 0:32] = second_tab[...]
-    heads_apart(first_query[...].astype(jnp.float32), mine32, 0)
-    heads_apart(second_query[...].astype(jnp.float32), mine32, 8)
+    for h in range(KVH):
+        part = queries[:, h * HD : (h + 1) * HD].astype(jnp.float32)
+        mine32[:, h, :] = part[:SESS]
+        mine32[:, 8 + h, :] = part[SESS:]
     for s in range(SESS):
-        token = first_fresh[s].astype(jnp.float32)
-        other = second_fresh[s].astype(jnp.float32)
+        first = tokens[s].astype(jnp.float32)
+        second = tokens[SESS + s].astype(jnp.float32)
         for h in range(KVH):
-            fr1[s, :, h, :] = token[:, h * HD : (h + 1) * HD]
-            for kv in range(2):
-                mine32[s, 16 + kv * 8 + h, :] = other[kv, h * HD : (h + 1) * HD]
+            fr1[s, :, h, :] = first[:, h * HD : (h + 1) * HD]
+            for row in range(2):
+                mine32[s, 16 + 8 * row + h, :] = second[row, h * HD : (h + 1) * HD]
     for s in range(SESS):
         mine[s] = mine32[s].astype(jnp.bfloat16)
 
@@ -158,7 +156,7 @@
     cross = []
     for r in (1, 2):
         cross.append(remote(mine, xmine.at[r - 1], x_ss.at[r - 1], x_rs.at[r - 1], at(-r)))
-        cross.append(remote(mytab, xtab.at[r - 1], x_ss.at[1 + r], x_rs.at[1 + r], at(-r)))
+        cross.append(remote(tabs.at[pl.ds(8, 8)], xtab.at[r - 1], x_ss.at[1 + r], x_rs.at[1 + r], at(-r)))
         cross.append(remote(meta, rmeta_ref.at[r - 1], x_ss.at[3 + r], x_rs.at[3 + r], at(r)))
     for copy in cross:
         copy.start()
@@ -239,12 +237,12 @@
     for r in (1, 2):
         a_code = codes[2 * r - 2 : 2 * r - 1, :]
         e_code = codes[2 * r - 1 : 2 * r, :]
-        left.append(jnp.minimum(jnp.max(jnp.where(first_tab[...] == a_code[:, :32], rows8[:SESS, :32], 0)), SESS - 1))
+        left.append(jnp.minimum(jnp.max(jnp.where(tabs[0:8, :] == a_code, rows8, 0)), SESS - 1))
         arrives.append(jnp.minimum(jnp.max(jnp.where(xtab[r - 1] == e_code, rows8, 0)), SESS - 1))
+
 
     relay_two(0, 2)
     relay_one(0, 2)
-
     lower = iota((16, 128), 0) >= 8
     for s in range(SESS):
         own = mine[s].astype(jnp.float32)
@@ -283,20 +281,15 @@
             lax.fori_loop(0, 16, one, 0, unroll=4)
 
     relay_two(2, 4)
-    relay_one(2, 3)
+    relay_one(2, 4)
     for u in range(1, N_TP):
         remote(
             qall.at[t], qall.at[peer(u)], q_ss.at[u], q_rs.at[peer(u)], (i, peer(u))
         ).wait_recv()
 
-    relay_two(4, HALF)
-
-    @pl.when(odd)
-    def _():
-        each(0, NBIG, lambda q: direct(2, q).start())
-
-    relay_one(3, 6)
-
+
+    relay_two(4, 6)
+    relay_one(4, 6)
     lane = iota((32, 128), 1)
     step_two = (iota((32, 128), 0) // 8) % 2
     lane_group = lane // 16
@@ -339,29 +332,23 @@
             @pl.when(2 * k + d != t)
             def _():
                 p_copy(2 * k + d).start()
-        relay_one(kk + 6, kk + 7)
+        relay_two(6 + kk * 2 // 8, 6 + (kk + 1) * 2 // 8)
+
+        @pl.when(odd & (kk == 7))
+        def _():
+            each(0, NBIG, lambda q: direct(2, q).start())
+
         return carry
 
     lax.fori_loop(0, KVH, head_step, 0)
-    relay_one(NCH - 2, NCH)
-
-    @pl.when(last)
-    def _():
-        each(0, NCH, lambda k: first_leg(1, k).wait_send())
-
-    @pl.when(y < 3)
-    def _():
-        each(0, NBIG, lambda q: direct(1, q).wait_send())
-
-    @pl.when(even)
-    def _():
-        each(NBIG // 2, NBIG, lambda q: direct(2, q).start())
-
+
+    relay_one(6, 10)
     for u in range(1, N_TP):
         remote(
             psend.at[t], prec.at[peer(u)], p_ss.at[t], p_rs.at[peer(u)], (i, peer(u))
         ).wait_recv()
     prec[t] = psend[t]
+    relay_one(10, 14)
     def top_step(u, best):
         return jnp.maximum(best, prec[u, SESS])
 
@@ -385,6 +372,20 @@
     for s in range(SESS):
         osc[s] = acc[s] / tot[s]
 
+    relay_one(14, 16)
+
+    @pl.when(last)
+    def _():
+        each(0, NCH, lambda k: first_leg(1, k).wait_send())
+
+    @pl.when(y < 3)
+    def _():
+        each(0, NBIG, lambda q: direct(1, q).wait_send())
+
+    @pl.when(even)
+    def _():
+        each(NBIG // 2, NBIG, lambda q: direct(2, q).start())
+
     for r in (0, 1):
         row = osc[left[r]]
         for s in range(SESS):
@@ -392,6 +393,30 @@
     outs = [remote(xsend.at[r], xrecv.at[r], o_ss.at[r], o_rs.at[r], at(r + 1)) for r in (0, 1)]
     for copy in outs:
         copy.start()
+    places = []
+    for step, lengths in enumerate((n1, n2)):
+        for s in range(SESS):
+            places.append((ints[8 * step + s, lengths[s] // PAGE] - low, lengths[s] % PAGE))
+    for l in range(SLOTS):
+        marks = []
+        for step in range(2):
+            sess, row = jnp.int32(0), jnp.int32(-1)
+            for s in range(SESS):
+                slot, at_row = places[step * SESS + s]
+                sess = jnp.where(slot == l, s, sess)
+                row = jnp.where(slot == l, at_row, row)
+            marks.append((sess, one_hot(row)))
+        (sess1, hot1), (sess2, hot2) = marks
+        keep = 1 - hot1 - hot2
+
+        def one(n, carry, l=l, sess1=sess1, sess2=sess2, hot1=hot1, hot2=hot2, keep=keep):
+            token1 = spread(fr1[sess1, n // 8, pl.ds(n % 8, 1), :])
+            token2 = spread(mine32[sess2, pl.ds(16 + n, 1), :])
+            tile = cbuf[l, n].reshape(8, 16, HD) * keep + token1 * hot1 + token2 * hot2
+            cbuf[l, n] = tile.reshape(PAGE, HD)
+            return carry
+
+        lax.fori_loop(0, 16, one, 0, unroll=4)
     for copy in outs:
         copy.wait_recv()
     for s in range(SESS):
@@ -437,7 +462,7 @@
         each(NBIG // 2, NBIG, lambda q: direct(2, q).wait_recv())
 
 
-def exchange(ft, n1, moves, st, first_query, second_query, first_fresh, second_fresh, cache):
+def exchange(ints, moves, queries, tokens, cache):
     vmem = pl.BlockSpec(memory_space=pltpu.VMEM)
     smem = pl.BlockSpec(memory_space=pltpu.SMEM)
     hbm = pl.BlockSpec(memory_space=pl.ANY)
@@ -450,17 +475,16 @@
             jax.ShapeDtypeStruct((SESS, 16, HD), f32),
             jax.ShapeDtypeStruct((2, TILES, PAGE, HD), bf16),
             jax.ShapeDtypeStruct((2, 8, 128), i32),
+            jax.ShapeDtypeStruct((SLOTS, 16, PAGE, HD), bf16),
         ),
-        in_specs=[smem, smem, smem] + [vmem] * 6 + [hbm],
-        out_specs=(vmem, hbm, vmem),
+        in_specs=[smem, vmem, vmem, vmem, vmem, hbm],
+        out_specs=(vmem, hbm, vmem, vmem),
         scratch_shapes=[
-            pltpu.VMEM((SLOTS, 16, PAGE, HD), bf16),
             pltpu.VMEM((2, TILES, PAGE, HD), bf16),
             pltpu.VMEM((TILES, PAGE, HD), bf16),
             pltpu.VMEM((2 * SESS, 16, PAGE, HD), bf16),
             pltpu.VMEM((8, 128), i32),
             pltpu.VMEM((N_TP, 8, 128), i32),
-            pltpu.VMEM((8, 128), i32),
             pltpu.VMEM((2, 8, 128), i32),
             pltpu.VMEM((SESS, 32, HD), f32),
             pltpu.VMEM((SESS, 2, 8, HD), f32),
@@ -484,56 +508,47 @@
             dma((NCH,)),
         ],
         compiler_params=pltpu.CompilerParams(
-            collective_id=1, has_side_effects=True, vmem_limit_bytes=56 * 1024 * 1024
+            collective_id=1, has_side_effects=True, vmem_limit_bytes=44 * 1024 * 1024
         ),
-    )(ft, n1, moves, ft, st, first_query, second_query, first_fresh, second_fresh, cache)
-
-
-def assemble_kernel(
-    came, ft, st, n1, n2, fresh1, fresh2, rows, cache, recv, first_out, second_out, out,
-    buf, in_sem, out_sem,
-):
+    )(ints, moves, ints, queries, tokens, cache)
+
+
+def assemble_kernel(came, ints, fresh, rows, kept, recv, first_out, second_out, out, buf, sem):
     low = lax.axis_index("tp") * SLOTS
     targets = [came[r, 4 + 2 * r + c, 0] for r in range(2) for c in range(2)]
-    for n, target in enumerate(targets):
+    for l in range(SLOTS):
+        hit = functools.reduce(jnp.logical_or, [target == l for target in targets])
+
+        @pl.when(jnp.logical_not(hit))
+        def _():
+            pltpu.make_async_copy(kept.at[l], out.at[l], sem.at[l]).start()
+    tokens = [fresh[SESS + s].astype(jnp.float32) for s in range(SESS)]
+    n2 = [ints[24, s] for s in range(SESS)]
+    for e, target in enumerate(targets):
+        row = jnp.int32(-1)
+        token = tokens[0]
+        for s in range(SESS):
+            hit = (ints[8 + s, n2[s] // PAGE] - low == target) & (target >= 0)
+            row = jnp.where(hit, n2[s] % PAGE, row)
+            token = jnp.where(hit, tokens[s], token)
+        hot = one_hot(row)
+        keep = 1 - hot
+        for n in range(16):
+            new = spread(token[n // 8 : n // 8 + 1, (n % 8) * HD : (n % 8 + 1) * HD])
+            tile = recv[e // 2, (e % 2) * 16 + n].reshape(8, 16, HD) * keep + new * hot
+            buf[e, n] = tile.reshape(PAGE, HD)
+
         @pl.when(target >= 0)
         def _():
-            pltpu.make_async_copy(
-                recv.at[n // 2, pl.ds((n % 2) * 16, 16)], buf.at[target], in_sem.at[target]
-            ).start()
-    for l in range(SLOTS):
-        hit = functools.reduce(jnp.logical_or, [target == l for target in targets])
-
-        @pl.when(jnp.logical_not(hit))
-        def _():
-            pltpu.make_async_copy(cache.at[l], buf.at[l], in_sem.at[l]).start()
+            pltpu.make_async_copy(buf.at[e], out.at[target], sem.at[target]).start()
     for h in range(KVH):
         first_out[:, h * HD : (h + 1) * HD] = rows[:, h, :].astype(first_out.dtype)
         second_out[:, h * HD : (h + 1) * HD] = rows[:, 8 + h, :].astype(second_out.dtype)
     for l in range(SLOTS):
-        pltpu.make_async_copy(cache.at[l], buf.at[l], in_sem.at[l]).wait()
-    for tables, lengths, fresh in ((ft, n1, fresh1), (st, n2, fresh2)):
-        for s in range(SESS):
-            slot = tables[s, lengths[s] // PAGE] - low
-            row = lengths[s] % PAGE
-
-            @pl.when((slot >= 0) & (slot < SLOTS))
-            def _():
-                start = pl.multiple_of((row // 16) * 16, 16)
-                put = iota((16, HD), 0) == row - start
-                token = fresh[s].astype(jnp.float32)
-                for n in range(16):
-                    new = token[n // 8 : n // 8 + 1, (n % 8) * HD : (n % 8 + 1) * HD]
-                    tile = buf[slot, n, pl.ds(start, 16), :].astype(jnp.float32)
-                    buf[slot, n, pl.ds(start, 16), :] = jnp.where(put, new, tile).astype(jnp.bfloat16)
-    outs = [pltpu.make_async_copy(buf.at[l], out.at[l], out_sem.at[l]) for l in range(SLOTS)]
-    for copy in outs:
-        copy.start()
-    for copy in outs:
-        copy.wait()
-
-
-def assemble(came, ft, st, n1, n2, fresh1, fresh2, rows, cache, recv):
+        pltpu.make_async_copy(kept.at[l], out.at[l], sem.at[l]).wait()
+
+
+def assemble(came, ints, fresh, rows, kept, recv):
     vmem = pl.BlockSpec(memory_space=pltpu.VMEM)
     hbm = pl.BlockSpec(memory_space=pl.ANY)
     smem = pl.BlockSpec(memory_space=pltpu.SMEM)
@@ -541,16 +556,15 @@
     return pl.pallas_call(
         assemble_kernel,
         name="assemble",
-        out_shape=(flat, flat, jax.ShapeDtypeStruct(cache.shape, cache.dtype)),
-        in_specs=[smem] * 5 + [vmem] * 3 + [hbm] * 2,
+        out_shape=(flat, flat, jax.ShapeDtypeStruct(kept.shape, kept.dtype)),
+        in_specs=[smem] * 2 + [vmem] * 2 + [hbm, vmem],
         out_specs=(vmem, vmem, hbm),
         scratch_shapes=[
-            pltpu.VMEM((SLOTS, 16, PAGE, HD), jnp.bfloat16),
-            pltpu.SemaphoreType.DMA((SLOTS,)),
+            pltpu.VMEM((4, 16, PAGE, HD), jnp.bfloat16),
             pltpu.SemaphoreType.DMA((SLOTS,)),
         ],
-        compiler_params=pltpu.CompilerParams(vmem_limit_bytes=56 * 1024 * 1024),
-    )(came, ft, st, n1, n2, fresh1, fresh2, rows, cache, recv)
+        compiler_params=pltpu.CompilerParams(vmem_limit_bytes=16 * 1024 * 1024),
+    )(came, ints, fresh, rows, kept, recv)
 
 
 def shards(
@@ -566,14 +580,20 @@
     page_moves,
 ):
     cache = cache_pool.reshape(SLOTS, 16, PAGE, HD)
-    rows, recv, came = exchange(
-        first_tables, first_lengths, page_moves, second_tables, first_query, second_query,
-        first_fresh, second_fresh, cache,
+    edge = ((0, 4), (0, 128 - first_tables.shape[1]))
+    line = ((0, 7), (0, 128 - SESS))
+    ints = jnp.concatenate(
+        [
+            jnp.pad(first_tables, edge, constant_values=-2),
+            jnp.pad(second_tables, edge, constant_values=-2),
+            jnp.pad(first_lengths[None], line),
+            jnp.pad(second_lengths[None], line),
+        ]
     )
-    first_out, second_out, cache_after = assemble(
-        came, first_tables, second_tables, first_lengths, second_lengths, first_fresh, second_fresh,
-        rows, cache, recv,
-    )
+    queries = jnp.concatenate([first_query, second_query])
+    tokens = jnp.concatenate([first_fresh, second_fresh])
+    rows, recv, came, kept = exchange(ints, page_moves, queries, tokens, cache)
+    first_out, second_out, cache_after = assemble(came, ints, tokens, rows, kept, recv)
     return first_out, second_out, cache_after.reshape(cache_pool.shape)
 
 

time: 73.2 us -> 66.9 us (0.914)
  Pallas kernels: 70.9 us -> 62 us
  other arithmetic: 0 us -> 1.46 us
  local copies, waits for them, and re-layouts: 1.36 us -> 2.24 us
    pallas_call x1, Pallas kernels: 63.6 us -> 57.7 us  [exchange(): pl.pallas_call(exchange_kernel, name='exchange', out_shape=(jax.ShapeDtyp...]
    pallas_call x1, Pallas kernels: 7.26 us -> 4.3 us  [assemble(): pl.pallas_call(assemble_kernel, name='assemble', out_shape=(flat, flat, j...]
    concatenate x0 -> x2, other arithmetic: none -> 1.46 us  [the longest x1 0.74 us: shards(): jnp.concatenate([jnp.pad(first_tables, edge, constant_values=-2), jnp.pad...]
    concatenate x0 -> x1, local copies, waits for them, and re-layouts: none -> 0.74 us  [shards(): tokens = jnp.concatenate([first_fresh, second_fresh])]
    unnamed x1 -> x2, local copies, waits for them, and re-layouts: 1.36 us -> 1.5 us
where the time goes in v3:
time: 66.9 us; the launch traced here: 66.4 us
  Pallas kernels  62 us (93%)
  local copies, waits for them, and re-layouts  2.24 us (3%)
  other arithmetic  1.46 us (2%)
    pallas_call x1, Pallas kernels, exchange(): pl.pallas_call(exchange_kernel, name='exchange', out_shape=(jax.ShapeDtyp...  57.7 us
    pallas_call x1, Pallas kernels, assemble(): pl.pallas_call(assemble_kernel, name='assemble', out_shape=(flat, flat, j...  4.3 us
    unnamed x2, local copies, waits for them, and re-layouts  1.5 us

profile of v3, /device:TPU:1, one launch (start us, length us, event | category | flops | bytes accessed | tf_op | source)
XLA Modules:
  0.0 66.4 jit_solution(17810779408486524252)
XLA Ops:
  0.6 0.8 %copy.13.moves = s32[1,8,2,2]{3,2,1,0:T(2,128)S(1)} copy(s32[1,8,2,2]{1,3,2,0:T(2,128)} %param.19) | data formatting | bytes 256 | tf_op args[9]
  1.4 0.7 %pad_add_fusion.ints.tabs = s32[32,128]{1,0:T(8,128)S(1)} fusion(s32[1,4]{1,0:T(1,128)} %bitcast.5, s32[1,4]{1,0:T(1,128)} %bitcast.6, s32[4,32]{1,0:T(4,128)} %param.16, s32[4,32]{1,0:T(4,128)} %param.15), kind=kLoop, calls=%fused_computation.2 | loop fusion | flops 36864 | bytes 17440 | tf_op jit(solution)/shard_map/concatenate | solution.py:585
  2.1 0.7 %pad_maximum_fusion.queries = bf16[8,1024]{1,0:T(8,128)(2,1)S(1)} fusion(bf16[4,1024]{1,0:T(4,128)(2,1)} %param.12, bf16[4,1024]{1,0:T(4,128)(2,1)} %param.11), kind=kLoop, calls=%fused_computation.6 | loop fusion | flops 32768 | bytes 32768 | tf_op jit(solution)/shard_map/concatenate | solution.py:593
  2.9 0.7 %constant_dynamic-update-slice_fusion.1 = bf16[8,2,1024]{2,1,0:T(2,128)(2,1)S(1)} fusion(bf16[4,2,1024]{2,1,0:T(2,128)(2,1)} %param.13), kind=kLoop, calls=%fused_computation.9 | loop fusion | bytes 32768
  3.6 0.7 %constant_dynamic-update-slice_fusion.tokens.fresh = bf16[8,2,1024]{2,1,0:T(2,128)(2,1)S(1)} fusion(bf16[8,2,1024]{2,1,0:T(2,128)(2,1)S(1)} %constant_dynamic-update-slice_fusion.1, bf16[4,2,1024]{2,1,0:T(2,128)(2,1)} %param.14), kind=kLoop, calls=%fused_computation.8 | loop fusion | bytes 32768 | tf_op jit(solution)/shard_map/concatenate | solution.py:594
  4.3 57.7 %exchange.1 = (f32[4,16,128]{2,1,0:T(8,128)S(1)}, bf16[2,32,128,128]{3,2,1,0:T(8,128)(2,1)S(1)}, s32[2,8,128]{2,1,0:T(8,128)S(1)}, bf16[12,16,128,128]{3,2,1,0:T(8,128)(2,1)S(1)}) custom-call(s32[32,128]{1,0:T(8,128)S(1)} %pad_add_fusion.ints.tabs, s32[1,8,2,2]{3,2,1,0:T(2,128)S(1)} %copy.13.moves, s32[32,128]{1,0:T(8,128)S(1)} %pad_add_fusion.ints.tabs, ...), custom_call_target="tpu_custom_call" | custom-call | tf_op jit(solution)/shard_map/exchange/pallas_call | solution.py:471
  62.1 4.3 %assemble.1 = (bf16[4,1024]{1,0:T(4,128)(2,1)}, bf16[4,1024]{1,0:T(4,128)(2,1)}, bf16[12,16,128,128]{3,2,1,0:T(8,128)(2,1)}) custom-call(s32[2,8,128]{2,1,0:T(8,128)S(1)} %get-tuple-element.10.came, s32[32,128]{1,0:T(8,128)S(1)} %pad_add_fusion.ints.tabs, bf16[8,2,1024]{2,1,0:T(2,128)(2,1)S(1)} %constant_dynamic-update-slice_fusion.tokens.fresh, ...), custom_call_target="tpu_custom_call" | custom-call | tf_op jit(solution)/shard_map/assemble/pallas_call | solution.py:556

commit v4 on v3

--- a/solution.py
+++ b/solution.py
@@ -38,7 +38,7 @@
 
 
 def exchange_kernel(
-    ints, moves, tabs, queries, tokens, cache,
+    ints, moves, tabs, floats, cache,
     out_ref, recv_ref, rmeta_ref, cbuf,
     pay, rel, pages, meta, metas, xtab, mine32, fr1, mine, xmine, fr2, qall, psend, prec,
     osc, xsend, xrecv,
@@ -108,17 +108,14 @@
         table = jnp.where(rows8 == 2 * r - 2, a_code, table)
         table = jnp.where(rows8 == 2 * r - 1, e_code, table)
     meta[...] = table
-    for h in range(KVH):
-        part = queries[:, h * HD : (h + 1) * HD].astype(jnp.float32)
-        mine32[:, h, :] = part[:SESS]
-        mine32[:, 8 + h, :] = part[SESS:]
     for s in range(SESS):
-        first = tokens[s].astype(jnp.float32)
-        second = tokens[SESS + s].astype(jnp.float32)
+        flat = floats[s].astype(jnp.float32)
         for h in range(KVH):
-            fr1[s, :, h, :] = first[:, h * HD : (h + 1) * HD]
+            part = flat[:, h * HD : (h + 1) * HD]
             for row in range(2):
-                mine32[s, 16 + 8 * row + h, :] = second[row, h * HD : (h + 1) * HD]
+                mine32[s, 8 * row + h, :] = part[row]
+                fr1[s, row, h, :] = part[2 + row]
+                mine32[s, 16 + 8 * row + h, :] = part[4 + row]
     for s in range(SESS):
         mine[s] = mine32[s].astype(jnp.bfloat16)
 
@@ -261,6 +258,11 @@
 
     for u in range(1, N_TP):
         q_copy(u).start()
+
+
+    @pl.when(odd)
+    def _():
+        each(0, 1, lambda q: direct(2, q).start())
 
     for s in range(SESS):
         for j in range(2):
@@ -332,11 +334,12 @@
             @pl.when(2 * k + d != t)
             def _():
                 p_copy(2 * k + d).start()
+
         relay_two(6 + kk * 2 // 8, 6 + (kk + 1) * 2 // 8)
 
         @pl.when(odd & (kk == 7))
         def _():
-            each(0, NBIG, lambda q: direct(2, q).start())
+            each(1, 4, lambda q: direct(2, q).start())
 
         return carry
 
@@ -372,20 +375,8 @@
     for s in range(SESS):
         osc[s] = acc[s] / tot[s]
 
+
     relay_one(14, 16)
-
-    @pl.when(last)
-    def _():
-        each(0, NCH, lambda k: first_leg(1, k).wait_send())
-
-    @pl.when(y < 3)
-    def _():
-        each(0, NBIG, lambda q: direct(1, q).wait_send())
-
-    @pl.when(even)
-    def _():
-        each(NBIG // 2, NBIG, lambda q: direct(2, q).start())
-
     for r in (0, 1):
         row = osc[left[r]]
         for s in range(SESS):
@@ -393,6 +384,19 @@
     outs = [remote(xsend.at[r], xrecv.at[r], o_ss.at[r], o_rs.at[r], at(r + 1)) for r in (0, 1)]
     for copy in outs:
         copy.start()
+
+    @pl.when(last)
+    def _():
+        each(0, NCH, lambda k: first_leg(1, k).wait_send())
+
+    @pl.when(y < 3)
+    def _():
+        each(0, NBIG, lambda q: direct(1, q).wait_send())
+
+    @pl.when(even)
+    def _():
+        each(NBIG // 2, NBIG, lambda q: direct(2, q).start())
+
     places = []
     for step, lengths in enumerate((n1, n2)):
         for s in range(SESS):
@@ -462,7 +466,7 @@
         each(NBIG // 2, NBIG, lambda q: direct(2, q).wait_recv())
 
 
-def exchange(ints, moves, queries, tokens, cache):
+def exchange(ints, moves, floats, cache):
     vmem = pl.BlockSpec(memory_space=pltpu.VMEM)
     smem = pl.BlockSpec(memory_space=pltpu.SMEM)
     hbm = pl.BlockSpec(memory_space=pl.ANY)
@@ -477,7 +481,7 @@
             jax.ShapeDtypeStruct((2, 8, 128), i32),
             jax.ShapeDtypeStruct((SLOTS, 16, PAGE, HD), bf16),
         ),
-        in_specs=[smem, vmem, vmem, vmem, vmem, hbm],
+        in_specs=[smem, vmem, vmem, vmem, hbm],
         out_specs=(vmem, hbm, vmem, vmem),
         scratch_shapes=[
             pltpu.VMEM((2, TILES, PAGE, HD), bf16),
@@ -510,10 +514,10 @@
         compiler_params=pltpu.CompilerParams(
             collective_id=1, has_side_effects=True, vmem_limit_bytes=44 * 1024 * 1024
         ),
-    )(ints, moves, ints, queries, tokens, cache)
-
-
-def assemble_kernel(came, ints, fresh, rows, kept, recv, first_out, second_out, out, buf, sem):
+    )(ints, moves, ints, floats, cache)
+
+
+def assemble_kernel(came, ints, floats, rows, kept, recv, first_out, second_out, out, buf, sem):
     low = lax.axis_index("tp") * SLOTS
     targets = [came[r, 4 + 2 * r + c, 0] for r in range(2) for c in range(2)]
     for l in range(SLOTS):
@@ -522,7 +526,7 @@
         @pl.when(jnp.logical_not(hit))
         def _():
             pltpu.make_async_copy(kept.at[l], out.at[l], sem.at[l]).start()
-    tokens = [fresh[SESS + s].astype(jnp.float32) for s in range(SESS)]
+    tokens = [floats[s, 4:6].astype(jnp.float32) for s in range(SESS)]
     n2 = [ints[24, s] for s in range(SESS)]
     for e, target in enumerate(targets):
         row = jnp.int32(-1)
@@ -548,7 +552,7 @@
         pltpu.make_async_copy(kept.at[l], out.at[l], sem.at[l]).wait()
 
 
-def assemble(came, ints, fresh, rows, kept, recv):
+def assemble(came, ints, floats, rows, kept, recv):
     vmem = pl.BlockSpec(memory_space=pltpu.VMEM)
     hbm = pl.BlockSpec(memory_space=pl.ANY)
     smem = pl.BlockSpec(memory_space=pltpu.SMEM)
@@ -564,7 +568,7 @@
             pltpu.SemaphoreType.DMA((SLOTS,)),
         ],
         compiler_params=pltpu.CompilerParams(vmem_limit_bytes=16 * 1024 * 1024),
-    )(came, ints, fresh, rows, kept, recv)
+    )(came, ints, floats, rows, kept, recv)
 
 
 def shards(
@@ -590,10 +594,17 @@
             jnp.pad(second_lengths[None], line),
         ]
     )
-    queries = jnp.concatenate([first_query, second_query])
-    tokens = jnp.concatenate([first_fresh, second_fresh])
-    rows, recv, came, kept = exchange(ints, page_moves, queries, tokens, cache)
-    first_out, second_out, cache_after = assemble(came, ints, tokens, rows, kept, recv)
+    shape = (SESS, 6, first_query.shape[1])
+    kind = lax.broadcasted_iota(jnp.int32, shape, 1)
+    floats = jnp.where(
+        kind < 4,
+        jnp.pad(first_fresh, ((0, 0), (2, 2), (0, 0))),
+        jnp.pad(second_fresh, ((0, 0), (4, 0), (0, 0))),
+    )
+    floats = jnp.where(kind == 0, lax.broadcast_in_dim(first_query, shape, (0, 2)), floats)
+    floats = jnp.where(kind == 1, lax.broadcast_in_dim(second_query, shape, (0, 2)), floats)
+    rows, recv, came, kept = exchange(ints, page_moves, floats, cache)
+    first_out, second_out, cache_after = assemble(came, ints, floats, rows, kept, recv)
     return first_out, second_out, cache_after.reshape(cache_pool.shape)
 
 

time: 66.9 us -> 60.8 us (0.909)
  Pallas kernels: 62 us -> 57.2 us
  local copies, waits for them, and re-layouts: 2.24 us -> 0.77 us
    pallas_call x1, Pallas kernels: 57.7 us -> 52.9 us  [exchange(): pl.pallas_call(exchange_kernel, name='exchange', out_shape=(jax.ShapeDtyp...]
    select_n x0 -> x1, other arithmetic: none -> 0.84 us  [shards(): jnp.where(kind == 1, lax.broadcast_in_dim(second_query, shape, (0, 2)), f...]
    concatenate x1 -> x0, local copies, waits for them, and re-layouts: 0.74 us -> none  [shards(): tokens = jnp.concatenate([first_fresh, second_fresh])]
    unnamed x2 -> x1, local copies, waits for them, and re-layouts: 1.5 us -> 0.77 us
    concatenate x1 -> x0, other arithmetic: 0.73 us -> none  [shards(): queries = jnp.concatenate([first_query, second_query])]
where the time goes in v4:
time: 60.8 us; the launch traced here: 60.3 us
  Pallas kernels  57.2 us (94%)
  other arithmetic  1.59 us (3%)
  local copies, waits for them, and re-layouts  0.77 us (1%)
  between operations  0.65 us (1%)
    pallas_call x1, Pallas kernels, exchange(): pl.pallas_call(exchange_kernel, name='exchange', out_shape=(jax.ShapeDtyp...  52.9 us
    pallas_call x1, Pallas kernels, assemble(): pl.pallas_call(assemble_kernel, name='assemble', out_shape=(flat, flat, j...  4.31 us

profile of v4, /device:TPU:1, one launch (start us, length us, event | category | flops | bytes accessed | tf_op | source)
XLA Modules:
  0.0 60.3 jit_solution(9369940164168963233)
XLA Ops:
  0.7 0.8 %copy.13.moves = s32[1,8,2,2]{3,2,1,0:T(2,128)S(1)} copy(s32[1,8,2,2]{1,3,2,0:T(2,128)} %param.19) | data formatting | bytes 256 | tf_op args[9]
  1.4 0.7 %pad_add_fusion.ints.tabs = s32[32,128]{1,0:T(8,128)S(1)} fusion(s32[1,4]{1,0:T(1,128)} %bitcast.5, s32[1,4]{1,0:T(1,128)} %bitcast.6, s32[4,32]{1,0:T(4,128)} %param.16, s32[4,32]{1,0:T(4,128)} %param.15), kind=kLoop, calls=%fused_computation.3 | loop fusion | flops 36864 | bytes 17440 | tf_op jit(solution)/shard_map/concatenate | solution.py:589
  2.2 0.8 %select_select_fusion.floats = bf16[4,6,1024]{2,1,0:T(8,128)(2,1)S(1)} fusion(bf16[4,2,1024]{2,1,0:T(2,128)(2,1)} %param.14, bf16[4,2,1024]{2,1,0:T(2,128)(2,1)} %param.13, pred[6]{0:T(512)(128)(4,1)S(1)} %get-tuple-element.17, pred[6]{0:T(512)(128)(4,1)S(1)} %get-tuple-element.18, pred[6]{0:T(512)(128)(4,1)S(1)} %iota_compare_fusion.5, ...), kind=kLoop, calls=%fused_computation | loop fusion | flops 73728 | bytes 98322 | tf_op jit(solution)/shard_map/jit(_where)/select_n | solution.py:605
  3.0 52.9 %exchange.1 = (f32[4,16,128]{2,1,0:T(8,128)S(1)}, bf16[2,32,128,128]{3,2,1,0:T(8,128)(2,1)S(1)}, s32[2,8,128]{2,1,0:T(8,128)S(1)}, bf16[12,16,128,128]{3,2,1,0:T(8,128)(2,1)S(1)}) custom-call(s32[32,128]{1,0:T(8,128)S(1)} %pad_add_fusion.ints.tabs, s32[1,8,2,2]{3,2,1,0:T(2,128)S(1)} %copy.13.moves, s32[32,128]{1,0:T(8,128)S(1)} %pad_add_fusion.ints.tabs, ...), custom_call_target="tpu_custom_call" | custom-call | tf_op jit(solution)/shard_map/exchange/pallas_call | solution.py:475
  56.0 4.3 %assemble.1 = (bf16[4,1024]{1,0:T(4,128)(2,1)}, bf16[4,1024]{1,0:T(4,128)(2,1)}, bf16[12,16,128,128]{3,2,1,0:T(8,128)(2,1)}) custom-call(s32[2,8,128]{2,1,0:T(8,128)S(1)} %get-tuple-element.10.came, s32[32,128]{1,0:T(8,128)S(1)} %pad_add_fusion.ints.tabs, bf16[4,6,1024]{2,1,0:T(8,128)(2,1)S(1)} %select_select_fusion.floats, ...), custom_call_target="tpu_custom_call" | custom-call | tf_op jit(solution)/shard_map/assemble/pallas_call | solution.py:560
  (2 shorter events, 0.0 us)

commit v5 on v4

--- a/solution.py
+++ b/solution.py
@@ -264,6 +264,11 @@
     def _():
         each(0, 1, lambda q: direct(2, q).start())
 
+
+    @pl.when(y == 0)
+    def _():
+        each(2, 4, lambda q: direct(2, q).start())
+
     for s in range(SESS):
         for j in range(2):
             e = s * 2 + j
@@ -292,6 +297,11 @@
 
     relay_two(4, 6)
     relay_one(4, 6)
+
+    @pl.when((y == 1))
+    def _():
+        each(1, 2, lambda q: direct(2, q).start())
+
     lane = iota((32, 128), 1)
     step_two = (iota((32, 128), 0) // 8) % 2
     lane_group = lane // 16
@@ -337,7 +347,12 @@
 
         relay_two(6 + kk * 2 // 8, 6 + (kk + 1) * 2 // 8)
 
-        @pl.when(odd & (kk == 7))
+        @pl.when((y == 1) & (kk == 7))
+        def _():
+            each(2, 4, lambda q: direct(2, q).start())
+
+
+        @pl.when((y == 3) & (kk == 7))
         def _():
             each(1, 4, lambda q: direct(2, q).start())
 
@@ -385,17 +400,9 @@
     for copy in outs:
         copy.start()
 
-    @pl.when(last)
-    def _():
-        each(0, NCH, lambda k: first_leg(1, k).wait_send())
-
-    @pl.when(y < 3)
-    def _():
-        each(0, NBIG, lambda q: direct(1, q).wait_send())
-
-    @pl.when(even)
-    def _():
-        each(NBIG // 2, NBIG, lambda q: direct(2, q).start())
+    @pl.when(y == 2)
+    def _():
+        each(2, 4, lambda q: direct(2, q).start())
 
     places = []
     for step, lengths in enumerate((n1, n2)):
@@ -421,6 +428,15 @@
             return carry
 
         lax.fori_loop(0, 16, one, 0, unroll=4)
+
+    @pl.when(last)
+    def _():
+        each(0, NCH, lambda k: first_leg(1, k).wait_send())
+
+    @pl.when(y < 3)
+    def _():
+        each(0, NBIG, lambda q: direct(1, q).wait_send())
+
     for copy in outs:
         copy.wait_recv()
     for s in range(SESS):

time: 60.8 us -> 60.8 us (level)
  no operation moved by 1% of the time
where the time goes in v5:
time: 60.8 us; the launch traced here: 59.9 us
  Pallas kernels  56.9 us (94%)
  other arithmetic  1.59 us (3%)
  local copies, waits for them, and re-layouts  0.77 us (1%)
  between operations  0.65 us (1%)
    pallas_call x1, Pallas kernels, exchange(): pl.pallas_call(exchange_kernel, name='exchange', out_shape=(jax.ShapeDtyp...  52.6 us
    pallas_call x1, Pallas kernels, assemble(): pl.pallas_call(assemble_kernel, name='assemble', out_shape=(flat, flat, j...  4.31 us

profile of v5, /device:TPU:1, one launch (start us, length us, event | category | flops | bytes accessed | tf_op | source)
XLA Modules:
  0.0 59.9 jit_solution(12442610235556348453)
XLA Ops:
  0.7 0.8 %copy.13.moves = s32[1,8,2,2]{3,2,1,0:T(2,128)S(1)} copy(s32[1,8,2,2]{1,3,2,0:T(2,128)} %param.19) | data formatting | bytes 256 | tf_op args[9]
  1.4 0.7 %pad_add_fusion.ints.tabs = s32[32,128]{1,0:T(8,128)S(1)} fusion(s32[1,4]{1,0:T(1,128)} %bitcast.5, s32[1,4]{1,0:T(1,128)} %bitcast.6, s32[4,32]{1,0:T(4,128)} %param.16, s32[4,32]{1,0:T(4,128)} %param.15), kind=kLoop, calls=%fused_computation.3 | loop fusion | flops 36864 | bytes 17440 | tf_op jit(solution)/shard_map/concatenate | solution.py:605
  2.2 0.8 %select_select_fusion.floats = bf16[4,6,1024]{2,1,0:T(8,128)(2,1)S(1)} fusion(bf16[4,2,1024]{2,1,0:T(2,128)(2,1)} %param.14, bf16[4,2,1024]{2,1,0:T(2,128)(2,1)} %param.13, pred[6]{0:T(512)(128)(4,1)S(1)} %get-tuple-element.17, pred[6]{0:T(512)(128)(4,1)S(1)} %get-tuple-element.18, pred[6]{0:T(512)(128)(4,1)S(1)} %iota_compare_fusion.5, ...), kind=kLoop, calls=%fused_computation | loop fusion | flops 73728 | bytes 98322 | tf_op jit(solution)/shard_map/jit(_where)/select_n | solution.py:621
  3.0 52.6 %exchange.1 = (f32[4,16,128]{2,1,0:T(8,128)S(1)}, bf16[2,32,128,128]{3,2,1,0:T(8,128)(2,1)S(1)}, s32[2,8,128]{2,1,0:T(8,128)S(1)}, bf16[12,16,128,128]{3,2,1,0:T(8,128)(2,1)S(1)}) custom-call(s32[32,128]{1,0:T(8,128)S(1)} %pad_add_fusion.ints.tabs, s32[1,8,2,2]{3,2,1,0:T(2,128)S(1)} %copy.13.moves, s32[32,128]{1,0:T(8,128)S(1)} %pad_add_fusion.ints.tabs, ...), custom_call_target="tpu_custom_call" | custom-call | tf_op jit(solution)/shard_map/exchange/pallas_call | solution.py:491
  55.6 4.3 %assemble.1 = (bf16[4,1024]{1,0:T(4,128)(2,1)}, bf16[4,1024]{1,0:T(4,128)(2,1)}, bf16[12,16,128,128]{3,2,1,0:T(8,128)(2,1)}) custom-call(s32[2,8,128]{2,1,0:T(8,128)S(1)} %get-tuple-element.10.came, s32[32,128]{1,0:T(8,128)S(1)} %pad_add_fusion.ints.tabs, bf16[4,6,1024]{2,1,0:T(8,128)(2,1)S(1)} %select_select_fusion.floats, ...), custom_call_target="tpu_custom_call" | custom-call | tf_op jit(solution)/shard_map/assemble/pallas_call | solution.py:576
  (2 shorter events, 0.0 us)

commit v6 on v5

--- a/solution.py
+++ b/solution.py
@@ -264,11 +264,6 @@
     def _():
         each(0, 1, lambda q: direct(2, q).start())
 
-
-    @pl.when(y == 0)
-    def _():
-        each(2, 4, lambda q: direct(2, q).start())
-
     for s in range(SESS):
         for j in range(2):
             e = s * 2 + j
@@ -298,9 +293,9 @@
     relay_two(4, 6)
     relay_one(4, 6)
 
-    @pl.when((y == 1))
-    def _():
-        each(1, 2, lambda q: direct(2, q).start())
+    @pl.when(y == 0)
+    def _():
+        each(2, 4, lambda q: direct(2, q).start())
 
     lane = iota((32, 128), 1)
     step_two = (iota((32, 128), 0) // 8) % 2
@@ -347,12 +342,7 @@
 
         relay_two(6 + kk * 2 // 8, 6 + (kk + 1) * 2 // 8)
 
-        @pl.when((y == 1) & (kk == 7))
-        def _():
-            each(2, 4, lambda q: direct(2, q).start())
-
-
-        @pl.when((y == 3) & (kk == 7))
+        @pl.when(odd & (kk == 7))
         def _():
             each(1, 4, lambda q: direct(2, q).start())
 
@@ -366,7 +356,7 @@
             psend.at[t], prec.at[peer(u)], p_ss.at[t], p_rs.at[peer(u)], (i, peer(u))
         ).wait_recv()
     prec[t] = psend[t]
-    relay_one(10, 14)
+    relay_one(10, 16)
     def top_step(u, best):
         return jnp.maximum(best, prec[u, SESS])
 
@@ -391,7 +381,6 @@
         osc[s] = acc[s] / tot[s]
 
 
-    relay_one(14, 16)
     for r in (0, 1):
         row = osc[left[r]]
         for s in range(SESS):

time: 60.8 us -> 60.8 us (level)
  no operation moved by 1% of the time
where the time goes in v6:
time: 60.8 us; the launch traced here: 59.9 us
  Pallas kernels  56.9 us (94%)
  other arithmetic  1.59 us (3%)
  local copies, waits for them, and re-layouts  0.77 us (1%)
  between operations  0.65 us (1%)
    pallas_call x1, Pallas kernels, exchange(): pl.pallas_call(exchange_kernel, name='exchange', out_shape=(jax.ShapeDtyp...  52.6 us
    pallas_call x1, Pallas kernels, assemble(): pl.pallas_call(assemble_kernel, name='assemble', out_shape=(flat, flat, j...  4.3 us

profile of v6, /device:TPU:1, one launch (start us, length us, event | category | flops | bytes accessed | tf_op | source)
XLA Modules:
  0.0 59.9 jit_solution(2057701386001259713)
XLA Ops:
  0.7 0.8 %copy.13.moves = s32[1,8,2,2]{3,2,1,0:T(2,128)S(1)} copy(s32[1,8,2,2]{1,3,2,0:T(2,128)} %param.19) | data formatting | bytes 256 | tf_op args[9]
  1.4 0.7 %pad_add_fusion.ints.tabs = s32[32,128]{1,0:T(8,128)S(1)} fusion(s32[1,4]{1,0:T(1,128)} %bitcast.5, s32[1,4]{1,0:T(1,128)} %bitcast.6, s32[4,32]{1,0:T(4,128)} %param.16, s32[4,32]{1,0:T(4,128)} %param.15), kind=kLoop, calls=%fused_computation.3 | loop fusion | flops 36864 | bytes 17440 | tf_op jit(solution)/shard_map/concatenate | solution.py:594
  2.2 0.8 %select_select_fusion.floats = bf16[4,6,1024]{2,1,0:T(8,128)(2,1)S(1)} fusion(bf16[4,2,1024]{2,1,0:T(2,128)(2,1)} %param.14, bf16[4,2,1024]{2,1,0:T(2,128)(2,1)} %param.13, pred[6]{0:T(512)(128)(4,1)S(1)} %get-tuple-element.17, pred[6]{0:T(512)(128)(4,1)S(1)} %get-tuple-element.18, pred[6]{0:T(512)(128)(4,1)S(1)} %iota_compare_fusion.5, ...), kind=kLoop, calls=%fused_computation | loop fusion | flops 73728 | bytes 98322 | tf_op jit(solution)/shard_map/jit(_where)/select_n | solution.py:610
  3.0 52.6 %exchange.1 = (f32[4,16,128]{2,1,0:T(8,128)S(1)}, bf16[2,32,128,128]{3,2,1,0:T(8,128)(2,1)S(1)}, s32[2,8,128]{2,1,0:T(8,128)S(1)}, bf16[12,16,128,128]{3,2,1,0:T(8,128)(2,1)S(1)}) custom-call(s32[32,128]{1,0:T(8,128)S(1)} %pad_add_fusion.ints.tabs, s32[1,8,2,2]{3,2,1,0:T(2,128)S(1)} %copy.13.moves, s32[32,128]{1,0:T(8,128)S(1)} %pad_add_fusion.ints.tabs, ...), custom_call_target="tpu_custom_call" | custom-call | tf_op jit(solution)/shard_map/exchange/pallas_call | solution.py:480
  55.6 4.3 %assemble.1 = (bf16[4,1024]{1,0:T(4,128)(2,1)}, bf16[4,1024]{1,0:T(4,128)(2,1)}, bf16[12,16,128,128]{3,2,1,0:T(8,128)(2,1)}) custom-call(s32[2,8,128]{2,1,0:T(8,128)S(1)} %get-tuple-element.10.came, s32[32,128]{1,0:T(8,128)S(1)} %pad_add_fusion.ints.tabs, bf16[4,6,1024]{2,1,0:T(8,128)(2,1)S(1)} %select_select_fusion.floats, ...), custom_call_target="tpu_custom_call" | custom-call | tf_op jit(solution)/shard_map/assemble/pallas_call | solution.py:565
  (2 shorter events, 0.0 us)
